TPU v7x, 512 devices: a whole 4x4x16 slice. The times are simulated.
512 devices in a mesh: ctx: 32 (over z, y_hi), tp: 16 (over y_lo, x, core).
Axes of the slice: x: 4, y: 4 (y_hi: 2, y_lo: 2; y = y_hi * 2 + y_lo), z: 16, core: 2. Of those that a mesh axis runs over, the one named last changes fastest.
Arguments:
- queries: bfloat16 [4096, 4096], P('ctx', 'tp'), may hold values from -10 to 10
- keys: bfloat16 [4096, 4096], P('ctx', 'tp'), may hold values from -10 to 10
- values: bfloat16 [4096, 4096], P('ctx', 'tp'), may hold values from -6 to 6
- attn_out: bfloat16 [4096, 4096], P('ctx', 'tp'), may hold values from -6 to 6
- out_grad: bfloat16 [4096, 6144], P('ctx', 'tp'), may hold values from -6 to 6
- out_weight: bfloat16 [4096, 6144], P('tp'), may hold values from -0.09375 to 0.09375
- token_sizes: int32 [4096], P('ctx'), may hold values from 1 to 16
Outputs:
- query_grad: bfloat16 [4096, 4096], P('ctx', 'tp')
- key_grad: bfloat16 [4096, 4096], P('ctx', 'tp')
- value_grad: bfloat16 [4096, 4096], P('ctx', 'tp')
All inputs are finite; a program needn't handle non-finite values.
Results may differ from a plain program's by a relative error of at most 0.0085.
Values may be sent and summed in bfloat16 or wider, within the bound.
A program may use at most 64 MiB of HBM per device.

v0:
```python
import jax
import jax.numpy as jnp
from jax import lax
from jax.sharding import PartitionSpec as P

HEADS = 32
HD = 128


def from_behind(block, axis, distance):
    devices = range(lax.axis_size(axis))
    route = [((i - distance) % len(devices), i) for i in devices]
    return lax.ppermute(block, axis, route)


def head_view(array, heads):
    return array.reshape(array.shape[0], heads, array.shape[1] // heads)


def block_terms(query, grad, lse, delta, key, value, bias):
    scale = 1.0 / HD**0.5
    scores = (
        scale * jnp.einsum("rhd,nhd->hrn", query, key, preferred_element_type=jnp.float32)
        + bias.astype(jnp.float32)[None, None, :]
    )
    probs = jnp.exp(scores - lse[:, :, None])
    probs_low = probs.astype(jnp.bfloat16)
    dprobs = jnp.einsum("rhd,nhd->hrn", grad, value, preferred_element_type=jnp.float32)
    dscores = (probs * (dprobs - delta[:, :, None])).astype(jnp.bfloat16)
    query_term = scale * jnp.einsum(
        "hrn,nhd->rhd", dscores, key, preferred_element_type=jnp.float32
    )
    key_term = scale * jnp.einsum(
        "hrn,rhd->nhd", dscores, query, preferred_element_type=jnp.float32
    )
    value_term = jnp.einsum("hrn,rhd->nhd", probs_low, grad, preferred_element_type=jnp.float32)
    return (query_term, key_term, value_term)


def pass_key_grads(key_acc, value_acc):
    return from_behind((key_acc, value_acc), "ctx", 1)


def local(queries, keys, values, attn_out, out_grad, out_weight, token_sizes):
    heads = HEADS // lax.axis_size("tp")
    rows = queries.shape[0]
    width = queries.shape[1]
    steps = lax.axis_size("ctx")
    scale = 1.0 / HD**0.5
    head_grad = lax.dot_general(
        lax.all_gather(out_grad, "tp", axis=1, tiled=True),
        out_weight,
        (((1,), (1,)), ((), ())),
        preferred_element_type=jnp.float32,
    ).astype(jnp.bfloat16)
    bias = jnp.log(token_sizes.astype(jnp.float32)).astype(jnp.bfloat16)
    query_heads = head_view(queries, heads)
    grad_heads = head_view(head_grad, heads)
    key_piece = lax.all_gather(keys, "ctx", axis=0, tiled=True)
    bias_piece = lax.all_gather(bias, "ctx", axis=0, tiled=True)
    scores = (
        scale
        * jnp.einsum(
            "rhd,nhd->hrn",
            query_heads,
            head_view(key_piece, heads),
            preferred_element_type=jnp.float32,
        )
        + bias_piece.astype(jnp.float32)[None, None, :]
    )
    highest = jnp.full((heads, rows), -1e30, jnp.float32)
    new_high = jnp.maximum(highest, jnp.max(scores, axis=-1))
    summed = jnp.sum(jnp.exp(scores - new_high[:, :, None]), axis=-1)
    highest, summed = (new_high, summed)
    lse = highest + jnp.log(summed)
    delta = jnp.einsum(
        "rhd,rhd->hr",
        grad_heads.astype(jnp.float32),
        head_view(attn_out, heads).astype(jnp.float32),
    )
    zeros = jnp.zeros((rows, heads, HD), jnp.float32)

    def visit(index, carry):
        moving, accs, query_acc = carry
        key_now, value_now, bias_now = moving
        query_term, key_term, value_term = block_terms(
            query_heads,
            grad_heads,
            lse,
            delta,
            head_view(key_now, heads),
            head_view(value_now, heads),
            bias_now,
        )
        moved = from_behind((key_now, value_now, bias_now), "ctx", 1)
        return (
            moved,
            pass_key_grads(accs[0] + key_term, accs[1] + value_term),
            query_acc + query_term,
        )

    moving, accs, query_acc = lax.fori_loop(
        0, steps - 1, visit, ((keys, values, bias), (zeros, zeros), zeros)
    )
    key_now, value_now, bias_now = moving
    query_term, key_term, value_term = block_terms(
        query_heads,
        grad_heads,
        lse,
        delta,
        head_view(key_now, heads),
        head_view(value_now, heads),
        bias_now,
    )
    key_acc, value_acc = pass_key_grads(accs[0] + key_term, accs[1] + value_term)
    query_acc = query_acc + query_term
    return (
        query_acc.reshape(rows, width).astype(jnp.bfloat16),
        key_acc.reshape(rows, width).astype(jnp.bfloat16),
        value_acc.reshape(rows, width).astype(jnp.bfloat16),
    )


def solution(mesh):
    in_specs = (
        P("ctx", "tp"),
        P("ctx", "tp"),
        P("ctx", "tp"),
        P("ctx", "tp"),
        P("ctx", "tp"),
        P("tp", None),
        P("ctx"),
    )
    out_specs = (P("ctx", "tp"), P("ctx", "tp"), P("ctx", "tp"))
    return jax.shard_map(local, mesh=mesh, in_specs=in_specs, out_specs=out_specs, check_vma=False)
```

profile of v0, /device:TPU:2, one launch (start us, length us, event | category | flops | bytes accessed | tf_op | source)
XLA Modules:
  0.0 1249.2 jit_solution(1714241333673851095)
XLA Ops:
  13.7 82.1 %all-gather = bf16[32,1,128]{2,1,0:T(2,128)(2,1)S(1)} all-gather(bf16[1,1,128]{2,1,0:T(2,128)(2,1)S(1)} %get-tuple-element.171), channel_id=1, replica_groups=mesh['ctx'=32,'tp'=16] {'ctx'}, dimensions={0}, use_global_device_ids=true | all-gather | bytes 8448 | tf_op jit(solution)/shard_map/all_gather | solution.py:60
  100.3 104.9 %all-gather.4.cloned.1.call-done = bf16[4096,256]{0,1:T(8,128)(2,1)} async-done(((bf16[128,256]{0,1:T(8,128)(2,1)}), bf16[4096,256]{0,1:T(8,128)(2,1)}) %all-gather.4.cloned.1.call-update) | async-done | bytes 2097168 | tf_op jit(solution)/shard_map/all_gather | solution.py:59
  209.1 1012.9 %while.21 = (s32[]{:T(128)}, bf16[128,256]{1,0:T(8,128)(2,1)}, bf16[128,256]{1,0:T(8,128)(2,1)}, bf16[128]{0:T(256)(128)(2,1)S(1)}, f32[128,2,128]{2,0,1:T(8,128...) while((s32[]{:T(128)}, bf16[128,256]{1,0:T(8,128)(2,1)}, ...), condition=%wide.region_3.0_spmd.clone, body=%wide.region_2.0_spmd.clone.sunk | while | flops 42369152 | bytes 3675215 | solution.py:102
  235.3 7.8 collective-permute-done.4
  267.8 7.1 collective-permute-done.4
  300.2 7.1 collective-permute-done.4
  332.7 7.1 collective-permute-done.4
  365.6 7.6 collective-permute-done.4
  386.5 6.8 collective-permute-start.3
  398.7 7.5 collective-permute-done.4
  419.4 6.8 collective-permute-start.3
  431.6 7.1 collective-permute-done.4
  463.8 7.1 collective-permute-done.4
  484.9 6.8 collective-permute-start.3
  497.1 7.2 collective-permute-done.4
  518.0 6.8 collective-permute-start.3
  530.3 7.1 collective-permute-done.4
  549.8 6.8 collective-permute-start.3
  562.1 7.1 collective-permute-done.4
  595.2 7.1 collective-permute-done.4
  626.7 7.1 collective-permute-done.4
  648.8 6.8 collective-permute-start.3
  661.0 7.1 collective-permute-done.4
  680.6 6.8 collective-permute-start.3
  692.8 7.1 collective-permute-done.4
  725.8 7.1 collective-permute-done.4
  758.0 7.1 collective-permute-done.4
  790.9 7.1 collective-permute-done.4
  822.7 8.0 collective-permute-done.4
  856.3 7.1 collective-permute-done.4
  887.4 7.1 collective-permute-done.4
  900.1 6.9 collective-permute-start.2
  922.1 7.1 collective-permute-done.4
  941.7 6.8 collective-permute-start.3
  954.0 7.2 collective-permute-done.4
  987.8 7.1 collective-permute-done.4
  1020.4 7.1 collective-permute-done.4
  1053.3 7.1 collective-permute-done.4
  1071.9 6.8 collective-permute-start.3
  1084.1 7.8 collective-permute-done.4
  1105.4 6.8 collective-permute-start.3
  1117.6 7.1 collective-permute-done.4
  1137.0 6.8 collective-permute-start.3
  1149.2 7.1 collective-permute-done.4
  1161.9 7.3 collective-permute-start.2
  1172.1 6.8 collective-permute-start.3
  1184.4 7.1 collective-permute-done.4
  1214.9 7.1 collective-permute-done.4
  (592 shorter events, 725.5 us)
Async XLA Ops:
  7.2 90.2 %all-gather.6.cloned.1.call-start = ((), (), s32[]{:S(2)}) async-start(), calls=%async_computation.1 | async-start | bytes 1671168 | tf_op jit(solution)/shard_map/all_gather | solution.py:51
  10.3 194.9 %all-gather.4.cloned.1.call-start = ((), (), s32[]{:S(2)}) async-start(), calls=%async_computation | async-start | bytes 2162688 | tf_op jit(solution)/shard_map/all_gather | solution.py:59
  210.0 25.2 %collective-permute-start = (bf16[128,256]{1,0:T(8,128)(2,1)S(1)}, bf16[128,256]{1,0:T(8,128)(2,1)}, u32[]{:S(2)}, u32[]{:S(2)}) collective-permute-start(bf16[128,256]{1,0:T(8,128)(2,1)S(1)} %copy.137), channel_id=1, source_target_pairs={{496,0},{0,16},{16,32},{32,48},{48,64},{64,80},{80,96},{96,112},{1... | collective-permute-start | bytes 196616 | tf_op jit(solution)/shard_map/while/body/eval_jaxpr/ppermute | solution.py:13
  243.9 23.9 %collective-permute-start = (bf16[128,256]{1,0:T(8,128)(2,1)S(1)}, bf16[128,256]{1,0:T(8,128)(2,1)}, u32[]{:S(2)}, u32[]{:S(2)}) collective-permute-start(bf16[128,256]{1,0:T(8,128)(2,1)S(1)} %copy.137), channel_id=1, source_target_pairs={{496,0},{0,16},{16,32},{32,48},{48,64},{64,80},{80,96},{96,112},{1... | collective-permute-start | bytes 196616 | tf_op jit(solution)/shard_map/while/body/eval_jaxpr/ppermute | solution.py:13
  275.8 24.4 %collective-permute-start = (bf16[128,256]{1,0:T(8,128)(2,1)S(1)}, bf16[128,256]{1,0:T(8,128)(2,1)}, u32[]{:S(2)}, u32[]{:S(2)}) collective-permute-start(bf16[128,256]{1,0:T(8,128)(2,1)S(1)} %copy.137), channel_id=1, source_target_pairs={{496,0},{0,16},{16,32},{32,48},{48,64},{64,80},{80,96},{96,112},{1... | collective-permute-start | bytes 196616 | tf_op jit(solution)/shard_map/while/body/eval_jaxpr/ppermute | solution.py:13
  308.2 24.6 %collective-permute-start = (bf16[128,256]{1,0:T(8,128)(2,1)S(1)}, bf16[128,256]{1,0:T(8,128)(2,1)}, u32[]{:S(2)}, u32[]{:S(2)}) collective-permute-start(bf16[128,256]{1,0:T(8,128)(2,1)S(1)} %copy.137), channel_id=1, source_target_pairs={{496,0},{0,16},{16,32},{32,48},{48,64},{64,80},{80,96},{96,112},{1... | collective-permute-start | bytes 196616 | tf_op jit(solution)/shard_map/while/body/eval_jaxpr/ppermute | solution.py:13
  340.7 24.9 %collective-permute-start = (bf16[128,256]{1,0:T(8,128)(2,1)S(1)}, bf16[128,256]{1,0:T(8,128)(2,1)}, u32[]{:S(2)}, u32[]{:S(2)}) collective-permute-start(bf16[128,256]{1,0:T(8,128)(2,1)S(1)} %copy.137), channel_id=1, source_target_pairs={{496,0},{0,16},{16,32},{32,48},{48,64},{64,80},{80,96},{96,112},{1... | collective-permute-start | bytes 196616 | tf_op jit(solution)/shard_map/while/body/eval_jaxpr/ppermute | solution.py:13
  343.4 22.1 %collective-permute-start.1 = (bf16[128,256]{1,0:T(8,128)(2,1)S(1)}, bf16[128,256]{1,0:T(8,128)(2,1)}, u32[]{:S(2)}, u32[]{:S(2)}) collective-permute-start(bf16[128,256]{1,0:T(8,128)(2,1)S(1)} %copy.138), channel_id=1, source_target_pairs={{496,0},{0,16},{16,32},{32,48},{48,64},{64,80},{80,96},{96,112},{1... | collective-permute-start | bytes 196616 | tf_op jit(solution)/shard_map/while/body/eval_jaxpr/ppermute | solution.py:13
  374.1 24.6 %collective-permute-start = (bf16[128,256]{1,0:T(8,128)(2,1)S(1)}, bf16[128,256]{1,0:T(8,128)(2,1)}, u32[]{:S(2)}, u32[]{:S(2)}) collective-permute-start(bf16[128,256]{1,0:T(8,128)(2,1)S(1)} %copy.137), channel_id=1, source_target_pairs={{496,0},{0,16},{16,32},{32,48},{48,64},{64,80},{80,96},{96,112},{1... | collective-permute-start | bytes 196616 | tf_op jit(solution)/shard_map/while/body/eval_jaxpr/ppermute | solution.py:13
  407.0 24.6 %collective-permute-start = (bf16[128,256]{1,0:T(8,128)(2,1)S(1)}, bf16[128,256]{1,0:T(8,128)(2,1)}, u32[]{:S(2)}, u32[]{:S(2)}) collective-permute-start(bf16[128,256]{1,0:T(8,128)(2,1)S(1)} %copy.137), channel_id=1, source_target_pairs={{496,0},{0,16},{16,32},{32,48},{48,64},{64,80},{80,96},{96,112},{1... | collective-permute-start | bytes 196616 | tf_op jit(solution)/shard_map/while/body/eval_jaxpr/ppermute | solution.py:13
  439.6 24.2 %collective-permute-start = (bf16[128,256]{1,0:T(8,128)(2,1)S(1)}, bf16[128,256]{1,0:T(8,128)(2,1)}, u32[]{:S(2)}, u32[]{:S(2)}) collective-permute-start(bf16[128,256]{1,0:T(8,128)(2,1)S(1)} %copy.137), channel_id=1, source_target_pairs={{496,0},{0,16},{16,32},{32,48},{48,64},{64,80},{80,96},{96,112},{1... | collective-permute-start | bytes 196616 | tf_op jit(solution)/shard_map/while/body/eval_jaxpr/ppermute | solution.py:13
  471.8 25.3 %collective-permute-start = (bf16[128,256]{1,0:T(8,128)(2,1)S(1)}, bf16[128,256]{1,0:T(8,128)(2,1)}, u32[]{:S(2)}, u32[]{:S(2)}) collective-permute-start(bf16[128,256]{1,0:T(8,128)(2,1)S(1)} %copy.137), channel_id=1, source_target_pairs={{496,0},{0,16},{16,32},{32,48},{48,64},{64,80},{80,96},{96,112},{1... | collective-permute-start | bytes 196616 | tf_op jit(solution)/shard_map/while/body/eval_jaxpr/ppermute | solution.py:13
  474.6 22.5 %collective-permute-start.1 = (bf16[128,256]{1,0:T(8,128)(2,1)S(1)}, bf16[128,256]{1,0:T(8,128)(2,1)}, u32[]{:S(2)}, u32[]{:S(2)}) collective-permute-start(bf16[128,256]{1,0:T(8,128)(2,1)S(1)} %copy.138), channel_id=1, source_target_pairs={{496,0},{0,16},{16,32},{32,48},{48,64},{64,80},{80,96},{96,112},{1... | collective-permute-start | bytes 196616 | tf_op jit(solution)/shard_map/while/body/eval_jaxpr/ppermute | solution.py:13
  505.2 25.0 %collective-permute-start = (bf16[128,256]{1,0:T(8,128)(2,1)S(1)}, bf16[128,256]{1,0:T(8,128)(2,1)}, u32[]{:S(2)}, u32[]{:S(2)}) collective-permute-start(bf16[128,256]{1,0:T(8,128)(2,1)S(1)} %copy.137), channel_id=1, source_target_pairs={{496,0},{0,16},{16,32},{32,48},{48,64},{64,80},{80,96},{96,112},{1... | collective-permute-start | bytes 196616 | tf_op jit(solution)/shard_map/while/body/eval_jaxpr/ppermute | solution.py:13
  508.0 22.3 %collective-permute-start.1 = (bf16[128,256]{1,0:T(8,128)(2,1)S(1)}, bf16[128,256]{1,0:T(8,128)(2,1)}, u32[]{:S(2)}, u32[]{:S(2)}) collective-permute-start(bf16[128,256]{1,0:T(8,128)(2,1)S(1)} %copy.138), channel_id=1, source_target_pairs={{496,0},{0,16},{16,32},{32,48},{48,64},{64,80},{80,96},{96,112},{1... | collective-permute-start | bytes 196616 | tf_op jit(solution)/shard_map/while/body/eval_jaxpr/ppermute | solution.py:13
  538.2 23.8 %collective-permute-start = (bf16[128,256]{1,0:T(8,128)(2,1)S(1)}, bf16[128,256]{1,0:T(8,128)(2,1)}, u32[]{:S(2)}, u32[]{:S(2)}) collective-permute-start(bf16[128,256]{1,0:T(8,128)(2,1)S(1)} %copy.137), channel_id=1, source_target_pairs={{496,0},{0,16},{16,32},{32,48},{48,64},{64,80},{80,96},{96,112},{1... | collective-permute-start | bytes 196616 | tf_op jit(solution)/shard_map/while/body/eval_jaxpr/ppermute | solution.py:13
  570.0 25.1 %collective-permute-start = (bf16[128,256]{1,0:T(8,128)(2,1)S(1)}, bf16[128,256]{1,0:T(8,128)(2,1)}, u32[]{:S(2)}, u32[]{:S(2)}) collective-permute-start(bf16[128,256]{1,0:T(8,128)(2,1)S(1)} %copy.137), channel_id=1, source_target_pairs={{496,0},{0,16},{16,32},{32,48},{48,64},{64,80},{80,96},{96,112},{1... | collective-permute-start | bytes 196616 | tf_op jit(solution)/shard_map/while/body/eval_jaxpr/ppermute | solution.py:13
  572.8 22.4 %collective-permute-start.1 = (bf16[128,256]{1,0:T(8,128)(2,1)S(1)}, bf16[128,256]{1,0:T(8,128)(2,1)}, u32[]{:S(2)}, u32[]{:S(2)}) collective-permute-start(bf16[128,256]{1,0:T(8,128)(2,1)S(1)} %copy.138), channel_id=1, source_target_pairs={{496,0},{0,16},{16,32},{32,48},{48,64},{64,80},{80,96},{96,112},{1... | collective-permute-start | bytes 196616 | tf_op jit(solution)/shard_map/while/body/eval_jaxpr/ppermute | solution.py:13
  603.1 23.6 %collective-permute-start = (bf16[128,256]{1,0:T(8,128)(2,1)S(1)}, bf16[128,256]{1,0:T(8,128)(2,1)}, u32[]{:S(2)}, u32[]{:S(2)}) collective-permute-start(bf16[128,256]{1,0:T(8,128)(2,1)S(1)} %copy.137), channel_id=1, source_target_pairs={{496,0},{0,16},{16,32},{32,48},{48,64},{64,80},{80,96},{96,112},{1... | collective-permute-start | bytes 196616 | tf_op jit(solution)/shard_map/while/body/eval_jaxpr/ppermute | solution.py:13
  634.7 26.3 %collective-permute-start = (bf16[128,256]{1,0:T(8,128)(2,1)S(1)}, bf16[128,256]{1,0:T(8,128)(2,1)}, u32[]{:S(2)}, u32[]{:S(2)}) collective-permute-start(bf16[128,256]{1,0:T(8,128)(2,1)S(1)} %copy.137), channel_id=1, source_target_pairs={{496,0},{0,16},{16,32},{32,48},{48,64},{64,80},{80,96},{96,112},{1... | collective-permute-start | bytes 196616 | tf_op jit(solution)/shard_map/while/body/eval_jaxpr/ppermute | solution.py:13
  637.5 23.5 %collective-permute-start.1 = (bf16[128,256]{1,0:T(8,128)(2,1)S(1)}, bf16[128,256]{1,0:T(8,128)(2,1)}, u32[]{:S(2)}, u32[]{:S(2)}) collective-permute-start(bf16[128,256]{1,0:T(8,128)(2,1)S(1)} %copy.138), channel_id=1, source_target_pairs={{496,0},{0,16},{16,32},{32,48},{48,64},{64,80},{80,96},{96,112},{1... | collective-permute-start | bytes 196616 | tf_op jit(solution)/shard_map/while/body/eval_jaxpr/ppermute | solution.py:13
  669.0 23.8 %collective-permute-start = (bf16[128,256]{1,0:T(8,128)(2,1)S(1)}, bf16[128,256]{1,0:T(8,128)(2,1)}, u32[]{:S(2)}, u32[]{:S(2)}) collective-permute-start(bf16[128,256]{1,0:T(8,128)(2,1)S(1)} %copy.137), channel_id=1, source_target_pairs={{496,0},{0,16},{16,32},{32,48},{48,64},{64,80},{80,96},{96,112},{1... | collective-permute-start | bytes 196616 | tf_op jit(solution)/shard_map/while/body/eval_jaxpr/ppermute | solution.py:13
  700.8 25.0 %collective-permute-start = (bf16[128,256]{1,0:T(8,128)(2,1)S(1)}, bf16[128,256]{1,0:T(8,128)(2,1)}, u32[]{:S(2)}, u32[]{:S(2)}) collective-permute-start(bf16[128,256]{1,0:T(8,128)(2,1)S(1)} %copy.137), channel_id=1, source_target_pairs={{496,0},{0,16},{16,32},{32,48},{48,64},{64,80},{80,96},{96,112},{1... | collective-permute-start | bytes 196616 | tf_op jit(solution)/shard_map/while/body/eval_jaxpr/ppermute | solution.py:13
  703.5 22.3 %collective-permute-start.1 = (bf16[128,256]{1,0:T(8,128)(2,1)S(1)}, bf16[128,256]{1,0:T(8,128)(2,1)}, u32[]{:S(2)}, u32[]{:S(2)}) collective-permute-start(bf16[128,256]{1,0:T(8,128)(2,1)S(1)} %copy.138), channel_id=1, source_target_pairs={{496,0},{0,16},{16,32},{32,48},{48,64},{64,80},{80,96},{96,112},{1... | collective-permute-start | bytes 196616 | tf_op jit(solution)/shard_map/while/body/eval_jaxpr/ppermute | solution.py:13
  733.8 24.3 %collective-permute-start = (bf16[128,256]{1,0:T(8,128)(2,1)S(1)}, bf16[128,256]{1,0:T(8,128)(2,1)}, u32[]{:S(2)}, u32[]{:S(2)}) collective-permute-start(bf16[128,256]{1,0:T(8,128)(2,1)S(1)} %copy.137), channel_id=1, source_target_pairs={{496,0},{0,16},{16,32},{32,48},{48,64},{64,80},{80,96},{96,112},{1... | collective-permute-start | bytes 196616 | tf_op jit(solution)/shard_map/while/body/eval_jaxpr/ppermute | solution.py:13
  766.0 24.9 %collective-permute-start = (bf16[128,256]{1,0:T(8,128)(2,1)S(1)}, bf16[128,256]{1,0:T(8,128)(2,1)}, u32[]{:S(2)}, u32[]{:S(2)}) collective-permute-start(bf16[128,256]{1,0:T(8,128)(2,1)S(1)} %copy.137), channel_id=1, source_target_pairs={{496,0},{0,16},{16,32},{32,48},{48,64},{64,80},{80,96},{96,112},{1... | collective-permute-start | bytes 196616 | tf_op jit(solution)/shard_map/while/body/eval_jaxpr/ppermute | solution.py:13
  768.8 22.1 %collective-permute-start.1 = (bf16[128,256]{1,0:T(8,128)(2,1)S(1)}, bf16[128,256]{1,0:T(8,128)(2,1)}, u32[]{:S(2)}, u32[]{:S(2)}) collective-permute-start(bf16[128,256]{1,0:T(8,128)(2,1)S(1)} %copy.138), channel_id=1, source_target_pairs={{496,0},{0,16},{16,32},{32,48},{48,64},{64,80},{80,96},{96,112},{1... | collective-permute-start | bytes 196616 | tf_op jit(solution)/shard_map/while/body/eval_jaxpr/ppermute | solution.py:13
  798.9 23.8 %collective-permute-start = (bf16[128,256]{1,0:T(8,128)(2,1)S(1)}, bf16[128,256]{1,0:T(8,128)(2,1)}, u32[]{:S(2)}, u32[]{:S(2)}) collective-permute-start(bf16[128,256]{1,0:T(8,128)(2,1)S(1)} %copy.137), channel_id=1, source_target_pairs={{496,0},{0,16},{16,32},{32,48},{48,64},{64,80},{80,96},{96,112},{1... | collective-permute-start | bytes 196616 | tf_op jit(solution)/shard_map/while/body/eval_jaxpr/ppermute | solution.py:13
  831.5 24.8 %collective-permute-start = (bf16[128,256]{1,0:T(8,128)(2,1)S(1)}, bf16[128,256]{1,0:T(8,128)(2,1)}, u32[]{:S(2)}, u32[]{:S(2)}) collective-permute-start(bf16[128,256]{1,0:T(8,128)(2,1)S(1)} %copy.137), channel_id=1, source_target_pairs={{496,0},{0,16},{16,32},{32,48},{48,64},{64,80},{80,96},{96,112},{1... | collective-permute-start | bytes 196616 | tf_op jit(solution)/shard_map/while/body/eval_jaxpr/ppermute | solution.py:13
  834.2 22.1 %collective-permute-start.1 = (bf16[128,256]{1,0:T(8,128)(2,1)S(1)}, bf16[128,256]{1,0:T(8,128)(2,1)}, u32[]{:S(2)}, u32[]{:S(2)}) collective-permute-start(bf16[128,256]{1,0:T(8,128)(2,1)S(1)} %copy.138), channel_id=1, source_target_pairs={{496,0},{0,16},{16,32},{32,48},{48,64},{64,80},{80,96},{96,112},{1... | collective-permute-start | bytes 196616 | tf_op jit(solution)/shard_map/while/body/eval_jaxpr/ppermute | solution.py:13
  864.3 23.1 %collective-permute-start = (bf16[128,256]{1,0:T(8,128)(2,1)S(1)}, bf16[128,256]{1,0:T(8,128)(2,1)}, u32[]{:S(2)}, u32[]{:S(2)}) collective-permute-start(bf16[128,256]{1,0:T(8,128)(2,1)S(1)} %copy.137), channel_id=1, source_target_pairs={{496,0},{0,16},{16,32},{32,48},{48,64},{64,80},{80,96},{96,112},{1... | collective-permute-start | bytes 196616 | tf_op jit(solution)/shard_map/while/body/eval_jaxpr/ppermute | solution.py:13
  895.4 26.7 %collective-permute-start = (bf16[128,256]{1,0:T(8,128)(2,1)S(1)}, bf16[128,256]{1,0:T(8,128)(2,1)}, u32[]{:S(2)}, u32[]{:S(2)}) collective-permute-start(bf16[128,256]{1,0:T(8,128)(2,1)S(1)} %copy.137), channel_id=1, source_target_pairs={{496,0},{0,16},{16,32},{32,48},{48,64},{64,80},{80,96},{96,112},{1... | collective-permute-start | bytes 196616 | tf_op jit(solution)/shard_map/while/body/eval_jaxpr/ppermute | solution.py:13
  898.1 24.0 %collective-permute-start.1 = (bf16[128,256]{1,0:T(8,128)(2,1)S(1)}, bf16[128,256]{1,0:T(8,128)(2,1)}, u32[]{:S(2)}, u32[]{:S(2)}) collective-permute-start(bf16[128,256]{1,0:T(8,128)(2,1)S(1)} %copy.138), channel_id=1, source_target_pairs={{496,0},{0,16},{16,32},{32,48},{48,64},{64,80},{80,96},{96,112},{1... | collective-permute-start | bytes 196616 | tf_op jit(solution)/shard_map/while/body/eval_jaxpr/ppermute | solution.py:13
  900.1 22.0 %collective-permute-start.2 = (bf16[128]{0:T(256)(128)(2,1)S(1)}, bf16[128]{0:T(256)(128)(2,1)S(1)}, u32[]{:S(2)}, u32[]{:S(2)}) collective-permute-start(bf16[128]{0:T(256)(128)(2,1)S(1)} %copy.139), channel_id=1, source_target_pairs={{496,0},{0,16},{16,32},{32,48},{48,64},{64,80},{80,96},{96,112},{1... | collective-permute-start | bytes 776 | tf_op jit(solution)/shard_map/while/body/eval_jaxpr/ppermute | solution.py:13
  930.1 23.9 %collective-permute-start = (bf16[128,256]{1,0:T(8,128)(2,1)S(1)}, bf16[128,256]{1,0:T(8,128)(2,1)}, u32[]{:S(2)}, u32[]{:S(2)}) collective-permute-start(bf16[128,256]{1,0:T(8,128)(2,1)S(1)} %copy.137), channel_id=1, source_target_pairs={{496,0},{0,16},{16,32},{32,48},{48,64},{64,80},{80,96},{96,112},{1... | collective-permute-start | bytes 196616 | tf_op jit(solution)/shard_map/while/body/eval_jaxpr/ppermute | solution.py:13
  962.1 25.8 %collective-permute-start = (bf16[128,256]{1,0:T(8,128)(2,1)S(1)}, bf16[128,256]{1,0:T(8,128)(2,1)}, u32[]{:S(2)}, u32[]{:S(2)}) collective-permute-start(bf16[128,256]{1,0:T(8,128)(2,1)S(1)} %copy.137), channel_id=1, source_target_pairs={{496,0},{0,16},{16,32},{32,48},{48,64},{64,80},{80,96},{96,112},{1... | collective-permute-start | bytes 196616 | tf_op jit(solution)/shard_map/while/body/eval_jaxpr/ppermute | solution.py:13
  964.8 23.0 %collective-permute-start.1 = (bf16[128,256]{1,0:T(8,128)(2,1)S(1)}, bf16[128,256]{1,0:T(8,128)(2,1)}, u32[]{:S(2)}, u32[]{:S(2)}) collective-permute-start(bf16[128,256]{1,0:T(8,128)(2,1)S(1)} %copy.138), channel_id=1, source_target_pairs={{496,0},{0,16},{16,32},{32,48},{48,64},{64,80},{80,96},{96,112},{1... | collective-permute-start | bytes 196616 | tf_op jit(solution)/shard_map/while/body/eval_jaxpr/ppermute | solution.py:13
  995.8 24.6 %collective-permute-start = (bf16[128,256]{1,0:T(8,128)(2,1)S(1)}, bf16[128,256]{1,0:T(8,128)(2,1)}, u32[]{:S(2)}, u32[]{:S(2)}) collective-permute-start(bf16[128,256]{1,0:T(8,128)(2,1)S(1)} %copy.137), channel_id=1, source_target_pairs={{496,0},{0,16},{16,32},{32,48},{48,64},{64,80},{80,96},{96,112},{1... | collective-permute-start | bytes 196616 | tf_op jit(solution)/shard_map/while/body/eval_jaxpr/ppermute | solution.py:13
  1028.4 24.9 %collective-permute-start = (bf16[128,256]{1,0:T(8,128)(2,1)S(1)}, bf16[128,256]{1,0:T(8,128)(2,1)}, u32[]{:S(2)}, u32[]{:S(2)}) collective-permute-start(bf16[128,256]{1,0:T(8,128)(2,1)S(1)} %copy.137), channel_id=1, source_target_pairs={{496,0},{0,16},{16,32},{32,48},{48,64},{64,80},{80,96},{96,112},{1... | collective-permute-start | bytes 196616 | tf_op jit(solution)/shard_map/while/body/eval_jaxpr/ppermute | solution.py:13
  1031.2 22.2 %collective-permute-start.1 = (bf16[128,256]{1,0:T(8,128)(2,1)S(1)}, bf16[128,256]{1,0:T(8,128)(2,1)}, u32[]{:S(2)}, u32[]{:S(2)}) collective-permute-start(bf16[128,256]{1,0:T(8,128)(2,1)S(1)} %copy.138), channel_id=1, source_target_pairs={{496,0},{0,16},{16,32},{32,48},{48,64},{64,80},{80,96},{96,112},{1... | collective-permute-start | bytes 196616 | tf_op jit(solution)/shard_map/while/body/eval_jaxpr/ppermute | solution.py:13
  1061.3 22.8 %collective-permute-start = (bf16[128,256]{1,0:T(8,128)(2,1)S(1)}, bf16[128,256]{1,0:T(8,128)(2,1)}, u32[]{:S(2)}, u32[]{:S(2)}) collective-permute-start(bf16[128,256]{1,0:T(8,128)(2,1)S(1)} %copy.137), channel_id=1, source_target_pairs={{496,0},{0,16},{16,32},{32,48},{48,64},{64,80},{80,96},{96,112},{1... | collective-permute-start | bytes 196616 | tf_op jit(solution)/shard_map/while/body/eval_jaxpr/ppermute | solution.py:13
  1092.8 24.8 %collective-permute-start = (bf16[128,256]{1,0:T(8,128)(2,1)S(1)}, bf16[128,256]{1,0:T(8,128)(2,1)}, u32[]{:S(2)}, u32[]{:S(2)}) collective-permute-start(bf16[128,256]{1,0:T(8,128)(2,1)S(1)} %copy.137), channel_id=1, source_target_pairs={{496,0},{0,16},{16,32},{32,48},{48,64},{64,80},{80,96},{96,112},{1... | collective-permute-start | bytes 196616 | tf_op jit(solution)/shard_map/while/body/eval_jaxpr/ppermute | solution.py:13
  1095.5 22.1 %collective-permute-start.1 = (bf16[128,256]{1,0:T(8,128)(2,1)S(1)}, bf16[128,256]{1,0:T(8,128)(2,1)}, u32[]{:S(2)}, u32[]{:S(2)}) collective-permute-start(bf16[128,256]{1,0:T(8,128)(2,1)S(1)} %copy.138), channel_id=1, source_target_pairs={{496,0},{0,16},{16,32},{32,48},{48,64},{64,80},{80,96},{96,112},{1... | collective-permute-start | bytes 196616 | tf_op jit(solution)/shard_map/while/body/eval_jaxpr/ppermute | solution.py:13
  1125.6 23.6 %collective-permute-start = (bf16[128,256]{1,0:T(8,128)(2,1)S(1)}, bf16[128,256]{1,0:T(8,128)(2,1)}, u32[]{:S(2)}, u32[]{:S(2)}) collective-permute-start(bf16[128,256]{1,0:T(8,128)(2,1)S(1)} %copy.137), channel_id=1, source_target_pairs={{496,0},{0,16},{16,32},{32,48},{48,64},{64,80},{80,96},{96,112},{1... | collective-permute-start | bytes 196616 | tf_op jit(solution)/shard_map/while/body/eval_jaxpr/ppermute | solution.py:13
  1157.2 27.2 %collective-permute-start = (bf16[128,256]{1,0:T(8,128)(2,1)S(1)}, bf16[128,256]{1,0:T(8,128)(2,1)}, u32[]{:S(2)}, u32[]{:S(2)}) collective-permute-start(bf16[128,256]{1,0:T(8,128)(2,1)S(1)} %copy.137), channel_id=1, source_target_pairs={{496,0},{0,16},{16,32},{32,48},{48,64},{64,80},{80,96},{96,112},{1... | collective-permute-start | bytes 196616 | tf_op jit(solution)/shard_map/while/body/eval_jaxpr/ppermute | solution.py:13
  1160.0 24.4 %collective-permute-start.1 = (bf16[128,256]{1,0:T(8,128)(2,1)S(1)}, bf16[128,256]{1,0:T(8,128)(2,1)}, u32[]{:S(2)}, u32[]{:S(2)}) collective-permute-start(bf16[128,256]{1,0:T(8,128)(2,1)S(1)} %copy.138), channel_id=1, source_target_pairs={{496,0},{0,16},{16,32},{32,48},{48,64},{64,80},{80,96},{96,112},{1... | collective-permute-start | bytes 196616 | tf_op jit(solution)/shard_map/while/body/eval_jaxpr/ppermute | solution.py:13
  1161.9 22.5 %collective-permute-start.2 = (bf16[128]{0:T(256)(128)(2,1)S(1)}, bf16[128]{0:T(256)(128)(2,1)S(1)}, u32[]{:S(2)}, u32[]{:S(2)}) collective-permute-start(bf16[128]{0:T(256)(128)(2,1)S(1)} %copy.139), channel_id=1, source_target_pairs={{496,0},{0,16},{16,32},{32,48},{48,64},{64,80},{80,96},{96,112},{1... | collective-permute-start | bytes 776 | tf_op jit(solution)/shard_map/while/body/eval_jaxpr/ppermute | solution.py:13
  1192.3 22.6 %collective-permute-start = (bf16[128,256]{1,0:T(8,128)(2,1)S(1)}, bf16[128,256]{1,0:T(8,128)(2,1)}, u32[]{:S(2)}, u32[]{:S(2)}) collective-permute-start(bf16[128,256]{1,0:T(8,128)(2,1)S(1)} %copy.137), channel_id=1, source_target_pairs={{496,0},{0,16},{16,32},{32,48},{48,64},{64,80},{80,96},{96,112},{1... | collective-permute-start | bytes 196616 | tf_op jit(solution)/shard_map/while/body/eval_jaxpr/ppermute | solution.py:13
  (114 other events, 2062.6 us)
Sparse Core Ops, SparseCore 0:
  10.5 45.0 all-gather.5
  59.0 146.2 all-gather.3
where the time goes:
time: 1260 us; the launch traced here: 1250 us
  starting transfers between devices  539 us (43%)
  waiting for transfers between devices  334 us (27%)
  matrix products  208 us (17%)
  blocking collectives  82.1 us (7%)
  local copies, waits for them, and re-layouts  67.2 us (5%)
  between operations  14.2 us (1%)
    ppermute x157, starting transfers between devices, from_behind(): return lax.ppermute(block, axis, route)  539 us
    ppermute x157, waiting for transfers between devices, from_behind(): return lax.ppermute(block, axis, route)  229 us
    all_gather x1, waiting for transfers between devices, local(): key_piece = lax.all_gather(keys, 'ctx', axis=0, tiled=True)  105 us
    all_gather x1, blocking collectives, local(): bias_piece = lax.all_gather(bias, 'ctx', axis=0, tiled=True)  82.1 us
    dot_general x32, matrix products, block_terms(): jnp.einsum('hrn,rhd->nhd', probs_low, grad, preferred_element_type=jnp.fl...  57 us
    dot_general x32, matrix products, block_terms(): jnp.einsum('hrn,rhd->nhd', dscores, query, preferred_element_type=jnp.flo...  54.8 us
    dot_general x32, matrix products, block_terms(): jnp.einsum('hrn,nhd->rhd', dscores, key, preferred_element_type=jnp.float32)  52.3 us
    while x93, local copies, waits for them, and re-layouts  52.2 us
  transfers between devices with their start and end apart: 159, of which 34 were waited for; matrix products, arithmetic and copies ran while one was open for 19% of the time, Pallas kernels for 0%

commit v1 on v0

v1 whole, which is shorter than its diff:
```python
import functools
import math

import jax
import jax.numpy as jnp
from jax import lax
from jax.experimental import pallas as pl
from jax.experimental.pallas import tpu as pltpu
from jax.sharding import PartitionSpec as P

MESH = pl.DeviceIdType.MESH
HD = 128
SCALE = 1.0 / HD**0.5
LOG2E = math.log2(math.e)
BF = jnp.bfloat16
F32 = jnp.float32
NT = (((1,), (1,)), ((), ()))
NN = (((1,), (0,)), ((), ()))
Q, K, V, G, BIAS, DELTA = range(6)
STAT = 6


def dot(a, b, dims):
    return lax.dot_general(a, b, dims, preferred_element_type=F32)


class Place:
    def __init__(self):
        self.c, self.t = lax.axis_index("ctx"), lax.axis_index("tp")
        self.z, self.yh = self.c // 2, self.c % 2
        self.yl, self.x, self.k = self.t // 8, (self.t % 8) // 2, self.t % 2
        self.y = self.yh * 2 + self.yl

    def other(self, d):
        return jnp.logical_or(d[0] != self.c, d[1] != self.t)

    def worker(self, piece, par):
        plane = self.x + 4 * (2 * self.k + par)
        return (plane * 2 + self.yh, (piece // 4) * 8 + (piece % 4) * 2 + self.yl)

    def home(self, s):
        return (s * 2 + self.yh, self.k * 8 + (self.z % 4) * 2 + self.z // 8)

    def along_x(self, j):
        return (self.c, self.yl * 8 + ((self.x + j) % 4) * 2 + self.k)

    def along_y(self, j):
        y = (self.y + j) % 4
        return (self.z * 2 + y // 2, (y % 2) * 8 + self.x * 2 + self.k)

    def chip(self, j):
        return (self.c, ((self.t // 2) ^ j) * 2 + self.k)

    def sibling(self):
        return (self.c, self.t + 1 - 2 * self.k)


def kernel(
    q_ref, k_ref, v_ref, o_ref, og_ref, w_ref, tok_ref, out_ref,
    og, w, qi, ki, vi, oi, gi, brow, dsend,
    qg, kg, vg, gg, bg, dg, st, e, ms, kt, bt, xb,
    dv, dk, dqo, rss, rsr, fin, outs,
    ld, p0s, p0r, a2s, a2r, ags, agr, rs_s, rs_r, ret_s, ret_r,
):
    me = Place()

    loads = [
        pltpu.make_async_copy(og_ref, og.at[:, pl.ds(pl.multiple_of(me.t * 384, 128), 384)], ld.at[0]),
        pltpu.make_async_copy(q_ref, qi, ld.at[1]),
        pltpu.make_async_copy(k_ref, ki, ld.at[2]),
        pltpu.make_async_copy(v_ref, vi, ld.at[3]),
        pltpu.make_async_copy(w_ref, w, ld.at[4]),
        pltpu.make_async_copy(o_ref, oi, ld.at[5]),
    ]
    barrier = pltpu.get_barrier_semaphore()
    partners = [me.home(s) for s in range(16)] + [me.worker(p, r) for p in range(8) for r in range(2)]
    partners += [me.chip(j) for j in range(1, 8)] + [me.sibling()]
    partners += [me.along_y(j) for j in range(1, 4)]
    expected = 0
    for d in partners:
        there = me.other(d)

        @pl.when(there)
        def _():
            pl.semaphore_signal(barrier, inc=1, device_id=d, device_id_type=MESH)

        expected = expected + there.astype(jnp.int32)
    for c in loads:
        c.start()
    brow[...] = jnp.log(tok_ref[...].astype(F32)).astype(BF).astype(F32)
    loads[0].wait()
    pl.semaphore_wait(barrier, expected)

    def remote(src, dst, s, r, d):
        return pltpu.make_async_remote_copy(src, dst, s, r, device_id=d, device_id_type=MESH)

    def og_at(slot):
        return og.at[:, pl.ds(pl.multiple_of(slot * 384, 128), 384)]

    mine = og_at(me.t)
    pushes = [remote(mine, mine, p0s.at[j], p0r.at[me.t], me.chip(j)) for j in range(1, 8)]
    pushes.append(remote(mine, mine, p0s.at[0], p0r.at[me.t], me.sibling()))
    for c in pushes:
        c.start()

    def spread(kind, src_of, dst_of):
        for p in range(8):
            for r in range(2):
                d = me.worker(p, r)
                src, dst = src_of(p, r), dst_of(p)
                send = remote(src, dst, a2s.at[kind, p * 2 + r], a2r.at[kind], d)
                keep = pltpu.make_async_copy(src, dst, a2r.at[kind])
                there = me.other(d)
                pl.when(there)(send.start)
                pl.when(jnp.logical_not(there))(keep.start)

    def spread_done(kind, src_of, dst_of):
        for p in range(8):
            for r in range(2):
                d = me.worker(p, r)
                send = remote(src_of(p, r), dst_of(p), a2s.at[kind, p * 2 + r], a2r.at[kind], d)
                pl.when(me.other(d))(send.wait_send)

    def part(a):
        return lambda p, r: a.at[pl.ds(p * 16, 16), pl.ds(r * 128, 128)]

    def slot_x(a):
        return lambda p: a.at[p % 4, pl.ds(pl.multiple_of(me.z * 16, 16), 16)]

    def slot_y(a):
        return lambda p: a.at[me.yh * 2 + p // 4, pl.ds(pl.multiple_of(me.z * 16, 16), 16)]

    routes = {
        Q: (part(qi), slot_x(qg)),
        K: (part(ki), slot_y(kg)),
        V: (part(vi), slot_y(vg)),
        G: (part(gi), slot_x(gg)),
        BIAS: (lambda p, r: brow, lambda p: bg.at[me.yh * 2 + p // 4, me.z]),
        DELTA: (lambda p, r: dsend.at[p * 2 + r], lambda p: dg.at[p % 4, me.z]),
    }
    for i, kind in ((1, Q), (2, K), (3, V)):
        loads[i].wait()
        spread(kind, *routes[kind])
        if kind == K:
            spread(BIAS, *routes[BIAS])

    acc = jnp.zeros((128, 256), F32)
    loads[4].wait()
    forwards = []
    for n, j in enumerate((0, 1, 3, 4, 5, 7, 2, 6)):
        chip = (me.t // 2) ^ j
        near, far = chip * 2 + me.k, chip * 2 + 1 - me.k
        if j:
            block = og_at(near)
            remote(block, block, p0s.at[0], p0r.at[near], me.sibling()).wait_recv()
            fwd = remote(block, block, p0s.at[8 + j], p0r.at[near], me.sibling())
            fwd.start()
            forwards.append(fwd)
        block = og_at(far)
        remote(block, block, p0s.at[0], p0r.at[far], me.sibling()).wait_recv()
        cols = pl.ds(pl.multiple_of(chip * 768, 128), 768)
        acc = acc + dot(og[:, cols], w[:, cols], NT)
    g = acc.astype(BF)
    gi[...] = g
    spread(G, *routes[G])

    loads[5].wait()
    prod = g.astype(F32) * oi[...].astype(F32)
    lane = lax.broadcasted_iota(jnp.int32, (8, 128), 1)
    keep = (lane // 16) == me.z % 8
    for r in range(2):
        row = jnp.sum(jnp.transpose(prod[:, r * 128 : (r + 1) * 128]), axis=0, keepdims=True)
        rows = pltpu.roll(jnp.broadcast_to(row, (8, 128)), (me.z % 8) * 16, 1)
        for p in range(8):
            turned = pltpu.roll(rows, (128 - p * 16) % 128, 1) if p else rows
            dsend[p * 2 + r] = jnp.where(keep, turned, 0.0)[0:1]
    spread(DELTA, *routes[DELTA])

    def arrived(kind, whole):
        pltpu.make_async_copy(whole, whole, a2r.at[kind]).wait()

    def share(kind, buf, slot, along):
        for j in (1, 3, 2):
            remote(buf.at[slot], buf.at[slot], ags.at[kind, j], agr.at[kind, slot], along(j)).start()

    def shared(kind, buf, slot):
        remote(buf.at[slot], buf.at[slot], ags.at[kind, 0], agr.at[kind, slot], me.sibling()).wait_recv()

    def share_done(kind, buf, slot, along):
        for j in (1, 3, 2):
            remote(buf.at[slot], buf.at[slot], ags.at[kind, j], agr.at[kind, slot], along(j)).wait_send()

    arrived(Q, qg.at[me.x])
    share(Q, qg, me.x, me.along_x)
    arrived(K, kg.at[me.y])
    share(K, kg, me.y, me.along_y)
    arrived(BIAS, bg.at[me.y])
    share(BIAS, bg, me.y, me.along_y)
    arrived(V, vg.at[me.y])
    share(V, vg, me.y, me.along_y)
    for j in (1, 3, 2):
        y = (me.y + j) % 4
        shared(BIAS, bg, y)
        shared(K, kg, y)
    sub = lax.broadcasted_iota(jnp.int32, (16, 128), 0)
    lane = lax.broadcasted_iota(jnp.int32, (16, 128), 1)
    for y in range(4):
        hit = lane == ((y % 2) * 4 + me.x) * 16 + sub
        for s in range(16):
            row = jnp.broadcast_to(bg[y, s], (16, 128))
            xb[pl.ds(y * 256 + s * 16, 16), :] = jnp.where(hit, row, 0.0).astype(BF)
    bt[...] = dot(xb[...], jnp.ones((128, 128), BF), NN) * LOG2E
    for y in range(4):
        kt[:, pl.ds(y * 256, 256)] = jnp.transpose(kg[y].astype(F32)).astype(BF)

    def score(j, carry):
        x = (me.x + j) % 4

        @pl.when(j > 0)
        def _():
            shared(Q, qg, x)

        keys = kg[...].reshape(1024, 128)
        bias = bt[...]
        s = dot(keys, qg[x], NT) * (SCALE * LOG2E) + jnp.concatenate([bias, bias], axis=1)
        m = jnp.max(s, axis=0, keepdims=True)
        p = jnp.exp2(s - m)
        e[x] = p
        ms[x] = m
        st[me.x, x] = m + jnp.log2(jnp.sum(p, axis=0, keepdims=True))
        return carry

    lax.fori_loop(0, 4, score, 0)
    share(STAT, st, me.x, me.along_x)

    arrived(G, gg.at[me.x])
    share(G, gg, me.x, me.along_x)
    arrived(DELTA, dg.at[me.x])
    share(DELTA, dg, me.x, me.along_x)
    for j in (1, 3, 2):
        shared(STAT, st, (me.x + j) % 4)
    for j in (1, 3, 2):
        shared(V, vg, (me.y + j) % 4)

    dv[...] = jnp.zeros_like(dv)
    dk[...] = jnp.zeros_like(dk)

    def grads(j, carry):
        x = (me.x + j) % 4

        @pl.when(j > 0)
        def _():
            shared(G, gg, x)
            shared(DELTA, dg, x)

        parts = [st[i, x] for i in range(4)]
        top = functools.reduce(jnp.maximum, parts)
        lse = top + jnp.log2(sum(jnp.exp2(a - top) for a in parts))
        p = e[x] * jnp.exp2(ms[x] - lse)
        grad = gg[x]
        dv[...] += dot(p.astype(BF), grad, NN)
        delta = jnp.concatenate([jnp.sum(dg[x, 0:8], axis=0), jnp.sum(dg[x, 8:16], axis=0)], axis=1)
        dp = dot(vg[...].reshape(1024, 128), grad, NT)
        ds = (p * (dp - delta)).astype(BF)
        dk[...] += dot(ds, qg[x], NN)
        dq = jnp.transpose(dot(kt[...], ds, NN)) * SCALE

        @pl.when(j == 0)
        def _():
            dqo[...] = dq

        @pl.when(j > 0)
        def _():
            rss[0, x] = dq.astype(BF)
            d = (me.c, me.yl * 8 + x * 2 + me.k)
            remote(rss.at[0, x], rsr.at[0, me.x], rs_s.at[0, x], rs_r.at[0, me.x], d).start()

        return carry

    lax.fori_loop(0, 4, grads, 0)

    for i, total in ((2, dv), (1, dk)):
        for j in (1, 3, 2):
            y = (me.y + j) % 4
            rows = total[pl.ds(pl.multiple_of(y * 256, 256), 256), :]
            rss[i, y] = (rows * SCALE if i == 1 else rows).astype(BF)
            remote(rss.at[i, y], rsr.at[i, me.y], rs_s.at[i, y], rs_r.at[i, me.y], me.along_y(j)).start()

    def give(i, s):
        piece = me.yl * 4 + me.x
        par = (me.z // 4) % 2
        dst = outs.at[
            i, pl.ds(pl.multiple_of(piece * 16, 16), 16), pl.ds(pl.multiple_of(par * 128, 128), 128)
        ]
        src = fin.at[i, pl.ds(s * 16, 16)]
        d = me.home(s)
        return (
            lambda: remote(src, dst, ret_s.at[i, s], ret_r.at[i], d),
            lambda: pltpu.make_async_copy(src, dst, ret_r.at[i]),
            me.other(d),
        )

    for i in (0, 2, 1):
        own = me.x if i == 0 else me.y
        if i == 0:
            total = dqo[...]
        else:
            total = (dv if i == 2 else dk)[pl.ds(pl.multiple_of(me.y * 256, 256), 256), :]
            total = total * SCALE if i == 1 else total
        for j in (1, 3, 2):
            n = (own + j) % 4
            remote(rsr.at[i, n], rsr.at[i, n], rs_s.at[i, 0], rs_r.at[i, n], me.sibling()).wait_recv()
            total = total + rsr[i, n].astype(F32)
        fin[i] = total.astype(BF)
        for s in range(16):
            send, stay, there = give(i, s)
            pl.when(there)(lambda: send().start())
            pl.when(jnp.logical_not(there))(lambda: stay().start())

    for c in pushes + forwards:
        c.wait_send()
    for kind, route in routes.items():
        spread_done(kind, *route)
    for kind, buf, slot, along in (
        (Q, qg, me.x, me.along_x),
        (K, kg, me.y, me.along_y),
        (V, vg, me.y, me.along_y),
        (G, gg, me.x, me.along_x),
        (BIAS, bg, me.y, me.along_y),
        (DELTA, dg, me.x, me.along_x),
        (STAT, st, me.x, me.along_x),
    ):
        share_done(kind, buf, slot, along)
    for i in range(3):
        own = me.x if i == 0 else me.y
        for j in (1, 3, 2):
            n = (own + j) % 4
            remote(rss.at[i, n], rsr.at[i, n], rs_s.at[i, n], rs_r.at[i, n], me.sibling()).wait_send()
        for s in range(16):
            send, stay, there = give(i, s)
            pl.when(there)(lambda: send().wait_send())
        pltpu.make_async_copy(outs.at[i], outs.at[i], ret_r.at[i]).wait()
    out_ref[...] = outs[...]


def split(a_ref, q_ref, k_ref, v_ref):
    q_ref[...] = a_ref[0]
    k_ref[...] = a_ref[1]
    v_ref[...] = a_ref[2]


def local(queries, keys, values, attn_out, out_grad, out_weight, token_sizes):
    any_ = pl.BlockSpec(memory_space=pl.ANY)
    vmem = pl.BlockSpec(memory_space=pltpu.VMEM)
    dma = pltpu.SemaphoreType.DMA
    scratch = [
        pltpu.VMEM((128, 6144), BF),
        pltpu.VMEM((256, 6144), BF),
        pltpu.VMEM((128, 256), BF),
        pltpu.VMEM((128, 256), BF),
        pltpu.VMEM((128, 256), BF),
        pltpu.VMEM((128, 256), BF),
        pltpu.VMEM((128, 256), BF),
        pltpu.VMEM((1, 128), F32),
        pltpu.VMEM((16, 1, 128), F32),
        pltpu.VMEM((4, 256, 128), BF),
        pltpu.VMEM((4, 256, 128), BF),
        pltpu.VMEM((4, 256, 128), BF),
        pltpu.VMEM((4, 256, 128), BF),
        pltpu.VMEM((4, 16, 1, 128), F32),
        pltpu.VMEM((4, 16, 1, 128), F32),
        pltpu.VMEM((4, 4, 1, 256), F32),
        pltpu.VMEM((4, 1024, 256), F32),
        pltpu.VMEM((4, 1, 256), F32),
        pltpu.VMEM((128, 1024), BF),
        pltpu.VMEM((1024, 128), F32),
        pltpu.VMEM((1024, 128), BF),
        pltpu.VMEM((1024, 128), F32),
        pltpu.VMEM((1024, 128), F32),
        pltpu.VMEM((256, 128), F32),
        pltpu.VMEM((3, 4, 256, 128), BF),
        pltpu.VMEM((3, 4, 256, 128), BF),
        pltpu.VMEM((3, 256, 128), BF),
        pltpu.VMEM((3, 128, 256), BF),
        dma((6,)),
        dma((16,)),
        dma((16,)),
        dma((6, 16)),
        dma((6,)),
        dma((7, 4)),
        dma((7, 4)),
        dma((3, 4)),
        dma((3, 4)),
        dma((3, 16)),
        dma((3,)),
    ]
    stacked = pl.pallas_call(
        kernel,
        out_shape=jax.ShapeDtypeStruct((3, 128, 256), BF),
        in_specs=[any_] * 6 + [vmem],
        out_specs=vmem,
        scratch_shapes=scratch,
        compiler_params=pltpu.CompilerParams(
            collective_id=0, has_side_effects=True, vmem_limit_bytes=48 * 2**20
        ),
        cost_estimate=pl.CostEstimate(flops=2 * 10**9, bytes_accessed=4 * 10**6, transcendentals=10**6),
        name="attention_backward",
    )(queries, keys, values, attn_out, out_grad, out_weight, token_sizes.reshape(1, 128))
    shape = jax.ShapeDtypeStruct((128, 256), BF)
    return pl.pallas_call(
        split,
        out_shape=(shape, shape, shape),
        in_specs=[vmem],
        out_specs=(vmem, vmem, vmem),
        name="split_outputs",
    )(stacked)


def solution(mesh):
    rows = P("ctx", "tp")
    return jax.shard_map(
        local,
        mesh=mesh,
        in_specs=(rows, rows, rows, rows, rows, P("tp", None), P("ctx")),
        out_specs=(rows, rows, rows),
        check_vma=False,
    )
```

time: 1260 us -> 86.7 us (0.07)
  the two profiles are of different devices: /device:TPU:2 before, /device:TPU:1 now
where the time goes in v1:
time: 86.7 us; the launch traced here: 86.3 us
  Pallas kernels  78.2 us (90%)
  local copies, waits for them, and re-layouts  7.45 us (9%)
    pallas_call x1, Pallas kernels, local(): pl.pallas_call(kernel, out_shape=jax.ShapeDtypeStruct((3, 128, 256), BF),...  76.6 us
    unnamed x16, local copies, waits for them, and re-layouts  7.45 us

profile of v1, /device:TPU:1, one launch (start us, length us, event | category | flops | bytes accessed | tf_op | source)
XLA Modules:
  0.0 86.3 jit_solution(2726869533729220305)
XLA Ops:
  0.6 0.0 copy-start.1
  0.6 1.9 %copy-done.1 = bf16[256,6144]{1,0:T(8,128)(2,1)S(1)} copy-done((bf16[256,6144]{1,0:T(8,128)(2,1)S(1)}, bf16[256,6144]{1,0:T(8,128)(2,1)}, u32[]{:S(2)}) %copy-start.1) | copy-done | bytes 3145752
  2.5 0.0 copy-start.2
  2.5 0.9 %copy-done.2 = bf16[128,384]{1,0:T(8,128)(2,1)S(1)} copy-done((bf16[128,384]{1,0:T(8,128)(2,1)S(1)}, bf16[128,384]{1,0:T(8,128)(2,1)}, u32[]{:S(2)}) %copy-start.2) | copy-done | bytes 98328
  3.4 0.0 copy-start.3
  3.4 0.8 copy-done.3
  4.3 0.0 copy-start.4
  4.3 0.8 copy-done.4
  5.1 0.0 copy-start.5
  5.1 0.8 copy-done.5
  5.9 0.0 copy-start.6
  5.9 0.8 copy-done.6
  6.8 0.0 copy-start.7
  6.8 0.7 copy-done.7
  7.4 76.6 %attention_backward.1.a_ref = bf16[3,128,256]{2,1,0:T(8,128)(2,1)S(1)} custom-call(bf16[128,256]{1,0:T(8,128)(2,1)S(1)} %copy-done.3, bf16[128,256]{1,0:T(8,128)(2,1)S(1)} %copy-done.4, bf16[128,256]{1,0:T(8,128)(2,1)S(1)} %copy-done.5, bf16[128,256]{1,0:T(8,128)(2,1)S(1)} %copy-done.6, bf16[128,384]{1,0:T(8,128)(2,1)S(1)} %copy-done.2, ...), custom_call_target="tpu_custom_call" | custom-call | flops 2000000000 | bytes 4000000 | tf_op jit(solution)/shard_map/attention_backward/pallas_call | solution.py:397
  84.0 0.0 copy-start
  84.0 0.7 copy-done
  84.7 1.6 %split_outputs.1 = (bf16[128,256]{1,0:T(8,128)(2,1)}, bf16[128,256]{1,0:T(8,128)(2,1)}, bf16[128,256]{1,0:T(8,128)(2,1)}) custom-call(bf16[3,128,256]{2,1,0:T(8,128)(2,1)} %copy-done), custom_call_target="tpu_custom_call" | custom-call | tf_op jit(solution)/shard_map/split_outputs/pallas_call | solution.py:410
Async XLA Ops:
  0.6 1.9 %copy-start.1 = (bf16[256,6144]{1,0:T(8,128)(2,1)S(1)}, bf16[256,6144]{1,0:T(8,128)(2,1)}, u32[]{:S(2)}) copy-start(bf16[256,6144]{1,0:T(8,128)(2,1)} %w_ref.1) | copy-start | bytes 9437188
  2.5 0.9 %copy-start.2 = (bf16[128,384]{1,0:T(8,128)(2,1)S(1)}, bf16[128,384]{1,0:T(8,128)(2,1)}, u32[]{:S(2)}) copy-start(bf16[128,384]{1,0:T(8,128)(2,1)} %og_ref.1) | copy-start | bytes 294916
  3.4 0.8 copy-start.3
  4.3 0.8 copy-start.4
  5.1 0.8 copy-start.5
  5.9 0.8 copy-start.6
  6.8 0.7 copy-start.7
  84.0 0.7 copy-start

commit v2 on v1

v2 whole, which is shorter than its diff:
```python
import functools
import math

import jax
import jax.numpy as jnp
from jax import lax
from jax.experimental import pallas as pl
from jax.experimental.pallas import tpu as pltpu
from jax.sharding import PartitionSpec as P

MESH = pl.DeviceIdType.MESH
HD = 128
SCALE = 1.0 / HD**0.5
LOG2E = math.log2(math.e)
BF = jnp.bfloat16
F32 = jnp.float32
NT = (((1,), (1,)), ((), ()))
NN = (((1,), (0,)), ((), ()))
Q, K, V, G, BIAS, DELTA = range(6)
STAT = 6


def dot(a, b, dims):
    return lax.dot_general(a, b, dims, preferred_element_type=F32)


class Place:
    def __init__(self):
        self.c, self.t = lax.axis_index("ctx"), lax.axis_index("tp")
        self.z, self.yh = self.c // 2, self.c % 2
        self.yl, self.x, self.k = self.t // 8, (self.t % 8) // 2, self.t % 2
        self.y = self.yh * 2 + self.yl

    def other(self, d):
        return jnp.logical_or(d[0] != self.c, d[1] != self.t)

    def worker(self, u):
        return (self.t * 2 + self.yh, u)

    def home(self, s):
        return (s * 2 + self.yh, self.z)

    def group(self, u):
        return (self.c, u)

    def column(self, s):
        return (s * 2 + self.yh, self.t)

    def along_x(self, j):
        return (self.c, self.yl * 8 + ((self.x + j) % 4) * 2 + self.k)

    def along_y(self, j):
        y = (self.y + j) % 4
        return (self.z * 2 + y // 2, (y % 2) * 8 + self.x * 2 + self.k)

    def chip(self, j):
        return (self.c, ((self.t // 2) ^ j) * 2 + self.k)

    def sibling(self):
        return (self.c, self.t + 1 - 2 * self.k)


def kernel(
    q_ref, k_ref, v_ref, o_ref, og_ref, w_ref, tok_ref, out_ref,
    og, w, qi, ki, vi, oi, gi, brow, dsend, relay, drelay,
    qg, kg, vg, gg, bg, dg, st, e, ms, kt, bt, xb,
    dv, dk, dqo, rss, rsr, fin, outs,
    ld, p0s, p0r, rls, rlr, a2s, a2r, ags, agr, rs_s, rs_r, ret_s, ret_r,
):
    me = Place()

    drains, pend = [], {}

    def finish():
        for wait in list(pend.values()) + drains:
            wait()
        out_ref[...] = outs[...]

    def remote(src, dst, s, r, d):
        return pltpu.make_async_remote_copy(src, dst, s, r, device_id=d, device_id_type=MESH)

    def landed(buf, sem):
        return lambda: pltpu.make_async_copy(buf, buf, sem).wait()

    def start(c):
        c.start()
        drains.append(c.wait_send)

    barrier = pltpu.get_barrier_semaphore()
    far = (8, 7, 9, 6, 10, 5, 11, 4, 12, 3, 13, 2, 14, 1, 15, 0)
    partners = [me.column((me.z + j) % 16) for j in far] + [me.home((me.z + j) % 16) for j in far]
    partners += [me.worker(u) for u in range(16)] + [me.group(u) for u in range(16)]
    partners += [(me.z * 2 + 1 - me.yh, l * 8 + me.x * 2 + me.k) for l in range(2)]
    expected = 0
    for d in partners:
        there = me.other(d)

        @pl.when(there)
        def _():
            pl.semaphore_signal(barrier, inc=1, device_id=d, device_id_type=MESH)

        expected = expected + there.astype(jnp.int32)

    def og_at(slot):
        return og.at[:, pl.ds(pl.multiple_of(slot * 384, 128), 384)]

    mine = og_at(me.t)
    loads = [
        pltpu.make_async_copy(src, dst, ld.at[i])
        for i, (src, dst) in enumerate(
            ((og_ref, mine), (q_ref, qi), (k_ref, ki), (v_ref, vi), (w_ref, w), (o_ref, oi))
        )
    ]
    for i, c in enumerate(loads):
        c.start()
        pend["load", i] = c.wait

    def loaded(i):
        pend.pop(("load", i))()

    brow[...] = jnp.log(tok_ref[...].astype(F32)).astype(BF).astype(F32)
    loaded(0)
    pl.semaphore_wait(barrier, expected)

    def send(src, dst, ss, rs, d):
        there = me.other(d)
        c = remote(src, dst, ss, rs, d)
        pl.when(there)(lambda: c.start())
        pl.when(jnp.logical_not(there))(lambda: pltpu.make_async_copy(src, dst, rs).start())
        drains.append(lambda: pl.when(there)(lambda: c.wait_send()))

    def part(a):
        return lambda u: a.at[pl.ds((u // 8 * 4 + u % 8 // 2) * 16, 16), pl.ds((u % 2) * 128, 128)]

    here = pl.ds(pl.multiple_of(me.z * 16, 16), 16)
    routes = {
        Q: (part(qi), relay.at[0], qg.at[me.x, here], qg.at[me.x]),
        K: (part(ki), relay.at[1], kg.at[me.y, here], kg.at[me.y]),
        V: (part(vi), relay.at[2], vg.at[me.y, here], vg.at[me.y]),
        G: (part(gi), relay.at[3], gg.at[me.x, here], gg.at[me.x]),
        DELTA: (lambda u: dsend.at[u], drelay, dg.at[me.x, me.z], dg.at[me.x]),
        BIAS: (None, None, bg.at[me.y, me.z], bg.at[me.y]),
    }

    def spread(kind):
        src, mid, _, _ = routes[kind]
        for u in range(16):
            send(src(u), mid.at[me.t], rls.at[kind, u], rlr.at[kind], me.group(u))
        pend["relay", kind] = landed(mid, rlr.at[kind])

    def climb(kind):
        _, mid, dst, whole = routes[kind]
        if mid is not None:
            pend.pop(("relay", kind))()
        for s in range(16):
            src = brow if mid is None else mid.at[s]
            send(src, dst, a2s.at[kind, s], a2r.at[kind], me.column(s))
        pend["a2a", kind] = landed(whole, a2r.at[kind])

    def arrived(kind):
        pend.pop(("a2a", kind))()

    for i, kind in ((1, Q), (2, K)):
        loaded(i)
        spread(kind)

    for j in range(1, 8):
        start(remote(mine, mine, p0s.at[j], p0r.at[me.t], me.chip(j)))
    start(remote(mine, mine, p0s.at[0], p0r.at[me.t], me.sibling()))
    for j in range(8):
        near = ((me.t // 2) ^ j) * 2 + me.k
        if j:
            pend["og", j] = landed(og_at(near), p0r.at[near])
        else:
            far = near + 1 - 2 * me.k
            pend["og", j] = landed(og_at(far), p0r.at[far])
    climb(BIAS)
    loaded(3)
    spread(V)
    climb(Q)
    climb(K)

    loaded(4)
    for key in [key for key in pend if key[0] == "og"]:
        del pend[key]
    acc = jnp.zeros((128, 256), F32)
    for j in (0, 1, 3, 4, 5, 7, 2, 6):
        chip = (me.t // 2) ^ j
        near, far = chip * 2 + me.k, chip * 2 + 1 - me.k
        if j:
            block = og_at(near)
            landed(block, p0r.at[near])()
            start(remote(block, block, p0s.at[8 + j], p0r.at[near], me.sibling()))
        landed(og_at(far), p0r.at[far])()
        cols = pl.ds(pl.multiple_of(chip * 768, 128), 768)
        acc = acc + dot(og[:, cols], w[:, cols], NT)
    g = acc.astype(BF)
    gi[...] = g
    spread(G)
    climb(V)
    climb(G)

    loaded(5)
    prod = g.astype(F32) * oi[...].astype(F32)
    lane = lax.broadcasted_iota(jnp.int32, (8, 128), 1)
    keep = (lane // 16) == me.z % 8
    for r in range(2):
        row = jnp.sum(jnp.transpose(prod[:, r * 128 : (r + 1) * 128]), axis=0, keepdims=True)
        rows = pltpu.roll(jnp.broadcast_to(row, (8, 128)), (me.z % 8) * 16, 1)
        for p in range(8):
            turned = pltpu.roll(rows, (128 - p * 16) % 128, 1) if p else rows
            dsend[p // 4 * 8 + p % 4 * 2 + r] = jnp.where(keep, turned, 0.0)[0:1]
    spread(DELTA)
    climb(DELTA)

    def share(kind, buf, own, along):
        for j in (1, 3, 2):
            start(remote(buf.at[own], buf.at[own], ags.at[kind, j], agr.at[kind, own], along(j)))
            n = (own + j) % 4
            pend["ag", kind, j] = landed(buf.at[n], agr.at[kind, n])

    def shared(kind):
        for j in (1, 3, 2):
            pend.pop(("ag", kind, j))()

    arrived(Q)
    share(Q, qg, me.x, me.along_x)
    arrived(K)
    share(K, kg, me.y, me.along_y)
    arrived(BIAS)
    share(BIAS, bg, me.y, me.along_y)
    arrived(V)
    share(V, vg, me.y, me.along_y)
    shared(BIAS)
    shared(K)
    sub = lax.broadcasted_iota(jnp.int32, (16, 128), 0)
    lane = lax.broadcasted_iota(jnp.int32, (16, 128), 1)
    for y in range(4):
        hit = lane == ((y % 2) * 4 + me.x) * 16 + sub
        for s in range(16):
            row = jnp.broadcast_to(bg[y, s], (16, 128))
            xb[pl.ds(y * 256 + s * 16, 16), :] = jnp.where(hit, row, 0.0).astype(BF)
    bt[...] = dot(xb[...], jnp.ones((128, 128), BF), NN) * LOG2E
    for y in range(4):
        kt[:, pl.ds(y * 256, 256)] = jnp.transpose(kg[y].astype(F32)).astype(BF)
    shared(Q)

    def score(j, carry):
        x = (me.x + j) % 4
        keys = kg[...].reshape(1024, 128)
        bias = bt[...]
        s = dot(keys, qg[x], NT) * (SCALE * LOG2E) + jnp.concatenate([bias, bias], axis=1)
        m = jnp.max(s, axis=0, keepdims=True)
        p = jnp.exp2(s - m)
        e[x] = p
        ms[x] = m
        st[me.x, x] = m + jnp.log2(jnp.sum(p, axis=0, keepdims=True))
        return carry

    lax.fori_loop(0, 4, score, 0)
    share(STAT, st, me.x, me.along_x)

    arrived(G)
    share(G, gg, me.x, me.along_x)
    arrived(DELTA)
    share(DELTA, dg, me.x, me.along_x)
    shared(STAT)
    shared(V)
    shared(G)
    shared(DELTA)

    dv[...] = jnp.zeros_like(dv)
    dk[...] = jnp.zeros_like(dk)

    def to_sum(i, own, n, d):
        return remote(rss.at[i, n], rsr.at[i, own], rs_s.at[i, n], rs_r.at[i, own], d)

    def grads(j, carry):
        x = (me.x + j) % 4
        parts = [st[i, x] for i in range(4)]
        top = functools.reduce(jnp.maximum, parts)
        lse = top + jnp.log2(sum(jnp.exp2(a - top) for a in parts))
        p = e[x] * jnp.exp2(ms[x] - lse)
        grad = gg[x]
        dv[...] += dot(p.astype(BF), grad, NN)
        delta = jnp.concatenate([jnp.sum(dg[x, 0:8], axis=0), jnp.sum(dg[x, 8:16], axis=0)], axis=1)
        dp = dot(vg[...].reshape(1024, 128), grad, NT)
        ds = (p * (dp - delta)).astype(BF)
        dk[...] += dot(ds, qg[x], NN)
        dq = jnp.transpose(dot(kt[...], ds, NN)) * SCALE

        @pl.when(j == 0)
        def _():
            dqo[...] = dq

        @pl.when(j > 0)
        def _():
            rss[0, x] = dq.astype(BF)
            to_sum(0, me.x, x, (me.c, me.yl * 8 + x * 2 + me.k)).start()

        return carry

    lax.fori_loop(0, 4, grads, 0)
    for i, own in ((0, me.x), (1, me.y), (2, me.y)):
        for j in (1, 3, 2):
            n = (own + j) % 4
            if i == 0:
                drains.append(to_sum(i, own, n, me.sibling()).wait_send)
                pend["rs", i, j] = landed(rsr.at[i, n], rs_r.at[i, n])

    for i, total in ((2, dv), (1, dk)):
        for j in (1, 3, 2):
            y = (me.y + j) % 4
            rows = total[pl.ds(pl.multiple_of(y * 256, 256), 256), :]
            rss[i, y] = (rows * SCALE if i == 1 else rows).astype(BF)
            start(to_sum(i, me.y, y, me.along_y(j)))
            pend["rs", i, j] = landed(rsr.at[i, y], rs_r.at[i, y])

    def give(i, act, act_self):
        piece = me.yl * 4 + me.x
        dst = outs.at[
            i, pl.ds(pl.multiple_of(piece * 16, 16), 16), pl.ds(pl.multiple_of(me.k * 128, 128), 128)
        ]
        for s in range(16):
            src = fin.at[i, pl.ds(s * 16, 16)]
            d = me.home(s)
            there = me.other(d)
            pl.when(there)(lambda: act(remote(src, dst, ret_s.at[i, s], ret_r.at[i], d)))
            if act_self:
                pl.when(jnp.logical_not(there))(lambda: pltpu.make_async_copy(src, dst, ret_r.at[i]).start())

    for i in (0, 2, 1):
        own = me.x if i == 0 else me.y
        if i == 0:
            total = dqo[...]
        else:
            total = (dv if i == 2 else dk)[pl.ds(pl.multiple_of(me.y * 256, 256), 256), :]
            total = total * SCALE if i == 1 else total
        for j in (1, 3, 2):
            pend.pop(("rs", i, j))()
            total = total + rsr[i, (own + j) % 4].astype(F32)
        fin[i] = total.astype(BF)
        give(i, lambda c: c.start(), True)
        drains.append(functools.partial(give, i, lambda c: c.wait_send(), False))
        pend["ret", i] = landed(outs.at[i], ret_r.at[i])
    finish()


def split(a_ref, q_ref, k_ref, v_ref, a, into, out):
    outs = (q_ref, k_ref, v_ref)
    first = [pltpu.make_async_copy(a_ref.at[i], a.at[i], into.at[i]) for i in range(3)]
    then = [pltpu.make_async_copy(a.at[i], outs[i], out.at[i]) for i in range(3)]
    for c in first:
        c.start()
    for c, d in zip(first, then):
        c.wait()
        d.start()
    for d in then:
        d.wait()


def local(queries, keys, values, attn_out, out_grad, out_weight, token_sizes):
    any_ = pl.BlockSpec(memory_space=pl.ANY)
    vmem = pl.BlockSpec(memory_space=pltpu.VMEM)
    dma = pltpu.SemaphoreType.DMA
    scratch = [
        pltpu.VMEM((128, 6144), BF),
        pltpu.VMEM((256, 6144), BF),
        pltpu.VMEM((128, 256), BF),
        pltpu.VMEM((128, 256), BF),
        pltpu.VMEM((128, 256), BF),
        pltpu.VMEM((128, 256), BF),
        pltpu.VMEM((128, 256), BF),
        pltpu.VMEM((1, 128), F32),
        pltpu.VMEM((16, 1, 128), F32),
        pltpu.VMEM((4, 16, 16, 128), BF),
        pltpu.VMEM((16, 1, 128), F32),
        pltpu.VMEM((4, 256, 128), BF),
        pltpu.VMEM((4, 256, 128), BF),
        pltpu.VMEM((4, 256, 128), BF),
        pltpu.VMEM((4, 256, 128), BF),
        pltpu.VMEM((4, 16, 1, 128), F32),
        pltpu.VMEM((4, 16, 1, 128), F32),
        pltpu.VMEM((4, 4, 1, 256), F32),
        pltpu.VMEM((4, 1024, 256), F32),
        pltpu.VMEM((4, 1, 256), F32),
        pltpu.VMEM((128, 1024), BF),
        pltpu.VMEM((1024, 128), F32),
        pltpu.VMEM((1024, 128), BF),
        pltpu.VMEM((1024, 128), F32),
        pltpu.VMEM((1024, 128), F32),
        pltpu.VMEM((256, 128), F32),
        pltpu.VMEM((3, 4, 256, 128), BF),
        pltpu.VMEM((3, 4, 256, 128), BF),
        pltpu.VMEM((3, 256, 128), BF),
        pltpu.VMEM((3, 128, 256), BF),
        dma((6,)),
        dma((16,)),
        dma((16,)),
        dma((6, 16)),
        dma((6,)),
        dma((6, 16)),
        dma((6,)),
        dma((7, 4)),
        dma((7, 4)),
        dma((3, 4)),
        dma((3, 4)),
        dma((3, 16)),
        dma((3,)),
    ]
    stacked = pl.pallas_call(
        kernel,
        out_shape=jax.ShapeDtypeStruct((3, 128, 256), BF),
        in_specs=[any_] * 6 + [vmem],
        out_specs=vmem,
        scratch_shapes=scratch,
        compiler_params=pltpu.CompilerParams(
            collective_id=0, has_side_effects=True, vmem_limit_bytes=62 * 2**20
        ),
        cost_estimate=pl.CostEstimate(flops=2 * 10**9, bytes_accessed=4 * 10**6, transcendentals=10**6),
        name="attention_backward",
    )(queries, keys, values, attn_out, out_grad, out_weight, token_sizes.reshape(1, 128))
    shape = jax.ShapeDtypeStruct((128, 256), BF)
    return pl.pallas_call(
        split,
        out_shape=(shape, shape, shape),
        in_specs=[any_],
        out_specs=(any_, any_, any_),
        scratch_shapes=[pltpu.VMEM((3, 128, 256), BF), dma((3,)), dma((3,))],
        compiler_params=pltpu.CompilerParams(vmem_limit_bytes=62 * 2**20),
        name="split_outputs",
    )(stacked)


def solution(mesh):
    rows = P("ctx", "tp")
    return jax.shard_map(
        local,
        mesh=mesh,
        in_specs=(rows, rows, rows, rows, rows, P("tp", None), P("ctx")),
        out_specs=(rows, rows, rows),
        check_vma=False,
    )
```

time: 86.7 us -> 82.5 us (0.952)
  local copies, waits for them, and re-layouts: 7.45 us -> 0 us
  Pallas kernels: 78.2 us -> 81.4 us
    unnamed x16 -> x0, local copies, waits for them, and re-layouts: 7.45 us -> none
    pallas_call x1, Pallas kernels: 76.6 us -> 79.8 us  [local(): pl.pallas_call(kernel, out_shape=jax.ShapeDtypeStruct((3, 128, 256), BF),...]
where the time goes in v2:
time: 82.5 us; the launch traced here: 82 us
  Pallas kernels  81.4 us (99%)
    pallas_call x1, Pallas kernels, local(): pl.pallas_call(kernel, out_shape=jax.ShapeDtypeStruct((3, 128, 256), BF),...  79.8 us

profile of v2, /device:TPU:1, one launch (start us, length us, event | category | flops | bytes accessed | tf_op | source)
XLA Modules:
  0.0 82.0 jit_solution(8359956013923484677)
XLA Ops:
  0.6 79.8 %attention_backward.1.a_ref = bf16[3,128,256]{2,1,0:T(8,128)(2,1)} custom-call(bf16[128,256]{1,0:T(8,128)(2,1)} %q_ref.1, bf16[128,256]{1,0:T(8,128)(2,1)} %k_ref.1, bf16[128,256]{1,0:T(8,128)(2,1)} %v_ref.1, bf16[128,256]{1,0:T(8,128)(2,1)} %o_ref.1, bf16[128,384]{1,0:T(8,128)(2,1)} %og_ref.1, bf16[256,6144]{1,0:T(8,128)(2,1)} %w_ref.1, s32[1,128]{1,0:T(1,128)} %bitcast.1), custom_call_target="tpu_custom_call" | custom-call | flops 2000000000 | bytes 4000000 | tf_op jit(solution)/shard_map/attention_backward/pallas_call | solution.py:411
  80.4 1.6 %split_outputs.1 = (bf16[128,256]{1,0:T(8,128)(2,1)}, bf16[128,256]{1,0:T(8,128)(2,1)}, bf16[128,256]{1,0:T(8,128)(2,1)}) custom-call(bf16[3,128,256]{2,1,0:T(8,128)(2,1)} %attention_backward.1.a_ref), custom_call_target="tpu_custom_call" | custom-call | tf_op jit(solution)/shard_map/split_outputs/pallas_call | solution.py:424

commit v3 on v2

--- a/solution.py
+++ b/solution.py
@@ -20,6 +20,10 @@
 STAT = 6
 
 
+def each(count, body):
+    lax.fori_loop(0, count, lambda i, c: (body(i), c)[1], 0)
+
+
 def dot(a, b, dims):
     return lax.dot_general(a, b, dims, preferred_element_type=F32)
 
@@ -62,10 +66,10 @@
 
 def kernel(
     q_ref, k_ref, v_ref, o_ref, og_ref, w_ref, tok_ref, out_ref,
-    og, w, qi, ki, vi, oi, gi, brow, dsend, relay, drelay,
+    og, w, qi, ki, vi, oi, gi, brow, drow, dsend, relay, drelay,
     qg, kg, vg, gg, bg, dg, st, e, ms, kt, bt, xb,
     dv, dk, dqo, rss, rsr, fin, outs,
-    ld, p0s, p0r, rls, rlr, a2s, a2r, ags, agr, rs_s, rs_r, ret_s, ret_r,
+    word, ld, p0s, p0r, rls, rlr, a2s, a2r, ags, agr, rs_s, rs_r, ret_s, ret_r,
 ):
     me = Place()
 
@@ -82,24 +86,26 @@
     def landed(buf, sem):
         return lambda: pltpu.make_async_copy(buf, buf, sem).wait()
 
-    def start(c):
-        c.start()
-        drains.append(c.wait_send)
-
     barrier = pltpu.get_barrier_semaphore()
-    far = (8, 7, 9, 6, 10, 5, 11, 4, 12, 3, 13, 2, 14, 1, 15, 0)
-    partners = [me.column((me.z + j) % 16) for j in far] + [me.home((me.z + j) % 16) for j in far]
-    partners += [me.worker(u) for u in range(16)] + [me.group(u) for u in range(16)]
-    partners += [(me.z * 2 + 1 - me.yh, l * 8 + me.x * 2 + me.k) for l in range(2)]
-    expected = 0
-    for d in partners:
-        there = me.other(d)
-
-        @pl.when(there)
-        def _():
-            pl.semaphore_signal(barrier, inc=1, device_id=d, device_id_type=MESH)
-
-        expected = expected + there.astype(jnp.int32)
+
+    def greet(d):
+        pl.semaphore_signal(barrier, inc=1, device_id=d, device_id_type=MESH)
+
+    each(15, lambda i: greet(me.group((me.t + i + 1) % 16)))
+    for l in range(2):
+        greet((me.z * 2 + 1 - me.yh, l * 8 + me.x * 2 + me.k))
+    for j in (1, 15):
+        greet(me.column((me.z + j) % 16))
+    expected = 19
+    apart = me.t != me.z
+
+    def tell(step):
+        for j in (2**step, 16 - 2**step):
+            d = me.column((me.z + j) % 16)
+            pl.semaphore_signal(word.at[step], inc=1, device_id=d, device_id_type=MESH)
+
+    def told(step):
+        pl.semaphore_wait(word.at[step], 2)
 
     def og_at(slot):
         return og.at[:, pl.ds(pl.multiple_of(slot * 384, 128), 384)]
@@ -121,16 +127,10 @@
     brow[...] = jnp.log(tok_ref[...].astype(F32)).astype(BF).astype(F32)
     loaded(0)
     pl.semaphore_wait(barrier, expected)
-
-    def send(src, dst, ss, rs, d):
-        there = me.other(d)
-        c = remote(src, dst, ss, rs, d)
-        pl.when(there)(lambda: c.start())
-        pl.when(jnp.logical_not(there))(lambda: pltpu.make_async_copy(src, dst, rs).start())
-        drains.append(lambda: pl.when(there)(lambda: c.wait_send()))
+    tell(0)
 
     def part(a):
-        return lambda u: a.at[pl.ds((u // 8 * 4 + u % 8 // 2) * 16, 16), pl.ds((u % 2) * 128, 128)]
+        return lambda u: a.at[pl.ds(pl.multiple_of((u // 8 * 4 + u % 8 // 2) * 16, 16), 16), pl.ds(pl.multiple_of((u % 2) * 128, 128), 128)]
 
     here = pl.ds(pl.multiple_of(me.z * 16, 16), 16)
     routes = {
@@ -144,17 +144,30 @@
 
     def spread(kind):
         src, mid, _, _ = routes[kind]
-        for u in range(16):
-            send(src(u), mid.at[me.t], rls.at[kind, u], rlr.at[kind], me.group(u))
+        pltpu.make_async_copy(src(me.t), mid.at[me.t], rlr.at[kind]).start()
+
+        def one(i):
+            u = (me.t + i + 1) % 16
+            remote(src(u), mid.at[me.t], rls.at[kind], rlr.at[kind], me.group(u)).start()
+
+        each(15, one)
+        drains.append(landed(mid.at[0:15], rls.at[kind]))
         pend["relay", kind] = landed(mid, rlr.at[kind])
 
     def climb(kind):
         _, mid, dst, whole = routes[kind]
+        src = (lambda s: brow) if mid is None else (lambda s: mid.at[s])
         if mid is not None:
             pend.pop(("relay", kind))()
-        for s in range(16):
-            src = brow if mid is None else mid.at[s]
-            send(src, dst, a2s.at[kind, s], a2r.at[kind], me.column(s))
+        pltpu.make_async_copy(src(me.z), dst, a2r.at[kind]).start()
+
+        def one(i):
+            s = (me.z + 1 + (i + 7) % 15) % 16
+            remote(src(s), dst, a2s.at[kind], a2r.at[kind], me.column(s)).start()
+
+        each(15, one)
+        sent = bg.at[0, 0:15] if mid is None else mid.at[0:15]
+        drains.append(landed(sent, a2s.at[kind]))
         pend["a2a", kind] = landed(whole, a2r.at[kind])
 
     def arrived(kind):
@@ -164,41 +177,54 @@
         loaded(i)
         spread(kind)
 
-    for j in range(1, 8):
-        start(remote(mine, mine, p0s.at[j], p0r.at[me.t], me.chip(j)))
-    start(remote(mine, mine, p0s.at[0], p0r.at[me.t], me.sibling()))
-    for j in range(8):
-        near = ((me.t // 2) ^ j) * 2 + me.k
-        if j:
-            pend["og", j] = landed(og_at(near), p0r.at[near])
-        else:
-            far = near + 1 - 2 * me.k
-            pend["og", j] = landed(og_at(far), p0r.at[far])
-    climb(BIAS)
+    def push(i):
+        remote(mine, mine, p0s.at[0], p0r.at[me.t], me.chip(i + 1)).start()
+
+    each(7, push)
+    remote(mine, mine, p0s.at[0], p0r.at[me.t], me.sibling()).start()
+    drains.append(landed(og.at[:, 0:3072], p0s.at[0]))
+    sib = me.t + 1 - 2 * me.k
+    pend["og", 0] = landed(og_at(sib), p0r.at[sib])
+
+    def pushed(i):
+        near = ((me.t // 2) ^ (i + 1)) * 2 + me.k
+        landed(og_at(near), p0r.at[near])()
+
+    pend["og", 1] = lambda: each(7, pushed)
     loaded(3)
     spread(V)
+    told(0)
+    tell(1)
+    told(1)
+    tell(2)
+    told(2)
+    climb(BIAS)
     climb(Q)
     climb(K)
 
     loaded(4)
     for key in [key for key in pend if key[0] == "og"]:
         del pend[key]
-    acc = jnp.zeros((128, 256), F32)
-    for j in (0, 1, 3, 4, 5, 7, 2, 6):
-        chip = (me.t // 2) ^ j
+    def features(chip):
+        cols = pl.ds(pl.multiple_of(chip * 768, 128), 768)
+        return dot(og[:, cols], w[:, cols], NT)
+
+    landed(og_at(sib), p0r.at[sib])()
+
+    def gather(i, acc):
+        chip = (me.t // 2) ^ (i + 1)
         near, far = chip * 2 + me.k, chip * 2 + 1 - me.k
-        if j:
-            block = og_at(near)
-            landed(block, p0r.at[near])()
-            start(remote(block, block, p0s.at[8 + j], p0r.at[near], me.sibling()))
+        block = og_at(near)
+        landed(block, p0r.at[near])()
+        remote(block, block, p0s.at[1], p0r.at[near], me.sibling()).start()
         landed(og_at(far), p0r.at[far])()
-        cols = pl.ds(pl.multiple_of(chip * 768, 128), 768)
-        acc = acc + dot(og[:, cols], w[:, cols], NT)
+        return acc + features(chip)
+
+    acc = lax.fori_loop(0, 7, gather, features(me.t // 2))
+    drains.append(landed(og.at[:, 0:2688], p0s.at[1]))
     g = acc.astype(BF)
     gi[...] = g
     spread(G)
-    climb(V)
-    climb(G)
 
     loaded(5)
     prod = g.astype(F32) * oi[...].astype(F32)
@@ -206,22 +232,33 @@
     keep = (lane // 16) == me.z % 8
     for r in range(2):
         row = jnp.sum(jnp.transpose(prod[:, r * 128 : (r + 1) * 128]), axis=0, keepdims=True)
-        rows = pltpu.roll(jnp.broadcast_to(row, (8, 128)), (me.z % 8) * 16, 1)
-        for p in range(8):
-            turned = pltpu.roll(rows, (128 - p * 16) % 128, 1) if p else rows
-            dsend[p // 4 * 8 + p % 4 * 2 + r] = jnp.where(keep, turned, 0.0)[0:1]
+        drow[r] = jnp.broadcast_to(row, (8, 128))
+
+    def lay(u):
+        piece = u // 8 * 4 + u % 8 // 2
+        rows = pltpu.roll(drow[u % 2], (me.z * 16 - piece * 16 + 256) % 128, 1)
+        dsend[u] = jnp.where(keep, rows, 0.0)[0:1]
+
+    each(16, lay)
     spread(DELTA)
+    climb(V)
+    climb(G)
     climb(DELTA)
 
     def share(kind, buf, own, along):
-        for j in (1, 3, 2):
-            start(remote(buf.at[own], buf.at[own], ags.at[kind, j], agr.at[kind, own], along(j)))
-            n = (own + j) % 4
-            pend["ag", kind, j] = landed(buf.at[n], agr.at[kind, n])
+        def one(i):
+            remote(buf.at[own], buf.at[own], ags.at[kind], agr.at[kind, own], along(i + 1)).start()
+
+        def wait(i):
+            n = (own + i + 1) % 4
+            landed(buf.at[n], agr.at[kind, n])()
+
+        each(3, one)
+        drains.append(landed(buf.at[0:3], ags.at[kind]))
+        pend["ag", kind] = lambda: each(3, wait)
 
     def shared(kind):
-        for j in (1, 3, 2):
-            pend.pop(("ag", kind, j))()
+        pend.pop(("ag", kind))()
 
     arrived(Q)
     share(Q, qg, me.x, me.along_x)
@@ -235,14 +272,19 @@
     shared(K)
     sub = lax.broadcasted_iota(jnp.int32, (16, 128), 0)
     lane = lax.broadcasted_iota(jnp.int32, (16, 128), 1)
-    for y in range(4):
-        hit = lane == ((y % 2) * 4 + me.x) * 16 + sub
-        for s in range(16):
-            row = jnp.broadcast_to(bg[y, s], (16, 128))
-            xb[pl.ds(y * 256 + s * 16, 16), :] = jnp.where(hit, row, 0.0).astype(BF)
+
+    def bias_rows(i):
+        hit = lane == ((i // 16 % 2) * 4 + me.x) * 16 + sub
+        row = jnp.broadcast_to(bg[i // 16, i % 16], (16, 128))
+        xb[pl.ds(pl.multiple_of(i * 16, 16), 16), :] = jnp.where(hit, row, 0.0).astype(BF)
+
+    each(64, bias_rows)
     bt[...] = dot(xb[...], jnp.ones((128, 128), BF), NN) * LOG2E
-    for y in range(4):
-        kt[:, pl.ds(y * 256, 256)] = jnp.transpose(kg[y].astype(F32)).astype(BF)
+
+    def turn(y):
+        kt[:, pl.ds(pl.multiple_of(y * 256, 256), 256)] = jnp.transpose(kg[y].astype(F32)).astype(BF)
+
+    each(4, turn)
     shared(Q)
 
     def score(j, carry):
@@ -265,35 +307,62 @@
     arrived(DELTA)
     share(DELTA, dg, me.x, me.along_x)
     shared(STAT)
-    shared(V)
-    shared(G)
-    shared(DELTA)
 
     dv[...] = jnp.zeros_like(dv)
     dk[...] = jnp.zeros_like(dk)
 
     def to_sum(i, own, n, d):
-        return remote(rss.at[i, n], rsr.at[i, own], rs_s.at[i, n], rs_r.at[i, own], d)
-
-    def grads(j, carry):
-        x = (me.x + j) % 4
+        return remote(rss.at[i, n], rsr.at[i, own], rs_s.at[i], rs_r.at[i, own], d)
+
+    def summed(i, own):
+        def wait(j):
+            n = (own + j + 1) % 4
+            landed(rsr.at[i, n], rs_r.at[i, n])()
+
+        drains.append(landed(rss.at[i, 0:3], rs_s.at[i]))
+        pend["rs", i] = lambda: each(3, wait)
+
+    def push_sums(i, total):
+        def one(j):
+            y = (me.y + j + 1) % 4
+            rows = total[pl.ds(pl.multiple_of(y * 256, 256), 256), :]
+            rss[i, y] = (rows * SCALE if i == 1 else rows).astype(BF)
+            to_sum(i, me.y, y, me.along_y(j + 1)).start()
+
+        each(3, one)
+        summed(i, me.y)
+
+    pend.pop(("ag", G))
+
+    def weigh(j, carry):
+        x = (me.x + (j ^ (j // 2))) % 4
+        pl.when(j > 0)(landed(gg.at[x], agr.at[G, x]))
         parts = [st[i, x] for i in range(4)]
         top = functools.reduce(jnp.maximum, parts)
         lse = top + jnp.log2(sum(jnp.exp2(a - top) for a in parts))
         p = e[x] * jnp.exp2(ms[x] - lse)
-        grad = gg[x]
-        dv[...] += dot(p.astype(BF), grad, NN)
+        e[x] = p
+        dv[...] += dot(p.astype(BF), gg[x], NN)
+        return carry
+
+    lax.fori_loop(0, 4, weigh, 0)
+    push_sums(2, dv)
+    shared(DELTA)
+    shared(V)
+
+    def grads(j, carry):
+        x = (me.x + 1 + j) % 4
         delta = jnp.concatenate([jnp.sum(dg[x, 0:8], axis=0), jnp.sum(dg[x, 8:16], axis=0)], axis=1)
-        dp = dot(vg[...].reshape(1024, 128), grad, NT)
-        ds = (p * (dp - delta)).astype(BF)
+        dp = dot(vg[...].reshape(1024, 128), gg[x], NT)
+        ds = (e[x] * (dp - delta)).astype(BF)
         dk[...] += dot(ds, qg[x], NN)
         dq = jnp.transpose(dot(kt[...], ds, NN)) * SCALE
 
-        @pl.when(j == 0)
+        @pl.when(j == 3)
         def _():
             dqo[...] = dq
 
-        @pl.when(j > 0)
+        @pl.when(j < 3)
         def _():
             rss[0, x] = dq.astype(BF)
             to_sum(0, me.x, x, (me.c, me.yl * 8 + x * 2 + me.k)).start()
@@ -301,48 +370,42 @@
         return carry
 
     lax.fori_loop(0, 4, grads, 0)
-    for i, own in ((0, me.x), (1, me.y), (2, me.y)):
-        for j in (1, 3, 2):
-            n = (own + j) % 4
-            if i == 0:
-                drains.append(to_sum(i, own, n, me.sibling()).wait_send)
-                pend["rs", i, j] = landed(rsr.at[i, n], rs_r.at[i, n])
-
-    for i, total in ((2, dv), (1, dk)):
-        for j in (1, 3, 2):
-            y = (me.y + j) % 4
-            rows = total[pl.ds(pl.multiple_of(y * 256, 256), 256), :]
-            rss[i, y] = (rows * SCALE if i == 1 else rows).astype(BF)
-            start(to_sum(i, me.y, y, me.along_y(j)))
-            pend["rs", i, j] = landed(rsr.at[i, y], rs_r.at[i, y])
-
-    def give(i, act, act_self):
+    summed(0, me.x)
+    push_sums(1, dk)
+
+    def give(i):
         piece = me.yl * 4 + me.x
         dst = outs.at[
             i, pl.ds(pl.multiple_of(piece * 16, 16), 16), pl.ds(pl.multiple_of(me.k * 128, 128), 128)
         ]
-        for s in range(16):
-            src = fin.at[i, pl.ds(s * 16, 16)]
-            d = me.home(s)
-            there = me.other(d)
-            pl.when(there)(lambda: act(remote(src, dst, ret_s.at[i, s], ret_r.at[i], d)))
-            if act_self:
-                pl.when(jnp.logical_not(there))(lambda: pltpu.make_async_copy(src, dst, ret_r.at[i]).start())
-
-    for i in (0, 2, 1):
+
+        def src(s):
+            return fin.at[i, pl.ds(pl.multiple_of(s * 16, 16), 16)]
+
+        def one(j):
+            s = (me.z + 1 + (j + 7) % 15) % 16
+            remote(src(s), dst, ret_s.at[i, 0], ret_r.at[i], me.home(s)).start()
+
+        each(15, one)
+        last = remote(src(me.z), dst, ret_s.at[i, 1], ret_r.at[i], me.home(me.z))
+        pl.when(apart)(lambda: last.start())
+        pl.when(jnp.logical_not(apart))(lambda: pltpu.make_async_copy(src(me.z), dst, ret_r.at[i]).start())
+        drains.append(landed(fin.at[i, 0:240], ret_s.at[i, 0]))
+        drains.append(lambda: pl.when(apart)(lambda: last.wait_send()))
+        pend["ret", i] = landed(outs.at[i], ret_r.at[i])
+
+    for i in (2, 0, 1):
         own = me.x if i == 0 else me.y
         if i == 0:
             total = dqo[...]
         else:
             total = (dv if i == 2 else dk)[pl.ds(pl.multiple_of(me.y * 256, 256), 256), :]
             total = total * SCALE if i == 1 else total
+        pend.pop(("rs", i))()
         for j in (1, 3, 2):
-            pend.pop(("rs", i, j))()
             total = total + rsr[i, (own + j) % 4].astype(F32)
         fin[i] = total.astype(BF)
-        give(i, lambda c: c.start(), True)
-        drains.append(functools.partial(give, i, lambda c: c.wait_send(), False))
-        pend["ret", i] = landed(outs.at[i], ret_r.at[i])
+        give(i)
     finish()
 
 
@@ -372,6 +435,7 @@
         pltpu.VMEM((128, 256), BF),
         pltpu.VMEM((128, 256), BF),
         pltpu.VMEM((1, 128), F32),
+        pltpu.VMEM((2, 8, 128), F32),
         pltpu.VMEM((16, 1, 128), F32),
         pltpu.VMEM((4, 16, 16, 128), BF),
         pltpu.VMEM((16, 1, 128), F32),
@@ -394,18 +458,19 @@
         pltpu.VMEM((3, 4, 256, 128), BF),
         pltpu.VMEM((3, 256, 128), BF),
         pltpu.VMEM((3, 128, 256), BF),
+        pltpu.SemaphoreType.REGULAR((3,)),
         dma((6,)),
+        dma((2,)),
         dma((16,)),
-        dma((16,)),
-        dma((6, 16)),
         dma((6,)),
-        dma((6, 16)),
         dma((6,)),
+        dma((6,)),
+        dma((6,)),
+        dma((7,)),
         dma((7, 4)),
-        dma((7, 4)),
+        dma((3,)),
         dma((3, 4)),
-        dma((3, 4)),
-        dma((3, 16)),
+        dma((3, 2)),
         dma((3,)),
     ]
     stacked = pl.pallas_call(

time: 82.5 us -> 75.4 us (0.914)
  the two profiles are of different devices: /device:TPU:1 before, /device:TPU:9 now
where the time goes in v3:
time: 75.4 us; the launch traced here: 75.3 us
  Pallas kernels  74.6 us (99%)
    pallas_call x1, Pallas kernels, local(): pl.pallas_call(kernel, out_shape=jax.ShapeDtypeStruct((3, 128, 256), BF),...  73 us
    pallas_call x1, Pallas kernels, local(): pl.pallas_call(split, out_shape=(shape, shape, shape), in_specs=[any_], o...  1.58 us

profile of v3, /device:TPU:9, one launch (start us, length us, event | category | flops | bytes accessed | tf_op | source)
XLA Modules:
  0.0 75.3 jit_solution(4482844573664984806)
XLA Ops:
  0.6 73.0 %attention_backward.1.a_ref = bf16[3,128,256]{2,1,0:T(8,128)(2,1)} custom-call(bf16[128,256]{1,0:T(8,128)(2,1)} %q_ref.1, bf16[128,256]{1,0:T(8,128)(2,1)} %k_ref.1, bf16[128,256]{1,0:T(8,128)(2,1)} %v_ref.1, bf16[128,256]{1,0:T(8,128)(2,1)} %o_ref.1, bf16[128,384]{1,0:T(8,128)(2,1)} %og_ref.1, bf16[256,6144]{1,0:T(8,128)(2,1)} %w_ref.1, s32[1,128]{1,0:T(1,128)} %bitcast.1), custom_call_target="tpu_custom_call" | custom-call | flops 2000000000 | bytes 4000000 | tf_op jit(solution)/shard_map/attention_backward/pallas_call | solution.py:476
  73.7 1.6 %split_outputs.1 = (bf16[128,256]{1,0:T(8,128)(2,1)}, bf16[128,256]{1,0:T(8,128)(2,1)}, bf16[128,256]{1,0:T(8,128)(2,1)}) custom-call(bf16[3,128,256]{2,1,0:T(8,128)(2,1)} %attention_backward.1.a_ref), custom_call_target="tpu_custom_call" | custom-call | tf_op jit(solution)/shard_map/split_outputs/pallas_call | solution.py:489

commit v4 on v3

--- a/solution.py
+++ b/solution.py
@@ -173,9 +173,12 @@
     def arrived(kind):
         pend.pop(("a2a", kind))()
 
-    for i, kind in ((1, Q), (2, K)):
-        loaded(i)
-        spread(kind)
+    loaded(1)
+    spread(Q)
+    told(0)
+    tell(1)
+    loaded(2)
+    spread(K)
 
     def push(i):
         remote(mine, mine, p0s.at[0], p0r.at[me.t], me.chip(i + 1)).start()
@@ -191,16 +194,20 @@
         landed(og_at(near), p0r.at[near])()
 
     pend["og", 1] = lambda: each(7, pushed)
-    loaded(3)
-    spread(V)
-    told(0)
-    tell(1)
-    told(1)
-    tell(2)
-    told(2)
-    climb(BIAS)
-    climb(Q)
-    climb(K)
+    def share(kind, buf, own, along):
+        def one(i):
+            remote(buf.at[own], buf.at[own], ags.at[kind], agr.at[kind, own], along(i + 1)).start()
+
+        def wait(i):
+            n = (own + i + 1) % 4
+            landed(buf.at[n], agr.at[kind, n])()
+
+        each(3, one)
+        drains.append(landed(buf.at[0:3], ags.at[kind]))
+        pend["ag", kind] = lambda: each(3, wait)
+
+    def shared(kind):
+        pend.pop(("ag", kind))()
 
     loaded(4)
     for key in [key for key in pend if key[0] == "og"]:
@@ -209,22 +216,32 @@
         cols = pl.ds(pl.multiple_of(chip * 768, 128), 768)
         return dot(og[:, cols], w[:, cols], NT)
 
-    landed(og_at(sib), p0r.at[sib])()
-
     def gather(i, acc):
-        chip = (me.t // 2) ^ (i + 1)
-        near, far = chip * 2 + me.k, chip * 2 + 1 - me.k
+        chip, last = (me.t // 2) ^ i, (me.t // 2) ^ (i - 1)
+        near, far = chip * 2 + me.k, last * 2 + 1 - me.k
         block = og_at(near)
         landed(block, p0r.at[near])()
         remote(block, block, p0s.at[1], p0r.at[near], me.sibling()).start()
         landed(og_at(far), p0r.at[far])()
-        return acc + features(chip)
-
-    acc = lax.fori_loop(0, 7, gather, features(me.t // 2))
+        return acc + features(last)
+
+    told(1)
+    tell(2)
+    loaded(3)
+    spread(V)
+    told(2)
+    climb(Q)
+    climb(K)
+    climb(BIAS)
+    acc = lax.fori_loop(1, 8, gather, jnp.zeros((128, 256), F32))
+    last = (me.t // 2) ^ 7
+    landed(og_at(last * 2 + 1 - me.k), p0r.at[last * 2 + 1 - me.k])()
+    acc = acc + features(last)
     drains.append(landed(og.at[:, 0:2688], p0s.at[1]))
     g = acc.astype(BF)
     gi[...] = g
     spread(G)
+    climb(V)
 
     loaded(5)
     prod = g.astype(F32) * oi[...].astype(F32)
@@ -241,35 +258,16 @@
 
     each(16, lay)
     spread(DELTA)
-    climb(V)
-    climb(G)
-    climb(DELTA)
-
-    def share(kind, buf, own, along):
-        def one(i):
-            remote(buf.at[own], buf.at[own], ags.at[kind], agr.at[kind, own], along(i + 1)).start()
-
-        def wait(i):
-            n = (own + i + 1) % 4
-            landed(buf.at[n], agr.at[kind, n])()
-
-        each(3, one)
-        drains.append(landed(buf.at[0:3], ags.at[kind]))
-        pend["ag", kind] = lambda: each(3, wait)
-
-    def shared(kind):
-        pend.pop(("ag", kind))()
-
     arrived(Q)
     share(Q, qg, me.x, me.along_x)
     arrived(K)
     share(K, kg, me.y, me.along_y)
     arrived(BIAS)
     share(BIAS, bg, me.y, me.along_y)
-    arrived(V)
-    share(V, vg, me.y, me.along_y)
+    climb(G)
+    climb(DELTA)
+
     shared(BIAS)
-    shared(K)
     sub = lax.broadcasted_iota(jnp.int32, (16, 128), 0)
     lane = lax.broadcasted_iota(jnp.int32, (16, 128), 1)
 
@@ -280,11 +278,7 @@
 
     each(64, bias_rows)
     bt[...] = dot(xb[...], jnp.ones((128, 128), BF), NN) * LOG2E
-
-    def turn(y):
-        kt[:, pl.ds(pl.multiple_of(y * 256, 256), 256)] = jnp.transpose(kg[y].astype(F32)).astype(BF)
-
-    each(4, turn)
+    shared(K)
     shared(Q)
 
     def score(j, carry):
@@ -299,13 +293,20 @@
         st[me.x, x] = m + jnp.log2(jnp.sum(p, axis=0, keepdims=True))
         return carry
 
+    arrived(G)
+    share(G, gg, me.x, me.along_x)
     lax.fori_loop(0, 4, score, 0)
     share(STAT, st, me.x, me.along_x)
 
-    arrived(G)
-    share(G, gg, me.x, me.along_x)
+    def turn(y):
+        kt[:, pl.ds(pl.multiple_of(y * 256, 256), 256)] = jnp.transpose(kg[y].astype(F32)).astype(BF)
+
+
     arrived(DELTA)
     share(DELTA, dg, me.x, me.along_x)
+    arrived(V)
+    share(V, vg, me.y, me.along_y)
+    each(4, turn)
     shared(STAT)
 
     dv[...] = jnp.zeros_like(dv)
@@ -350,29 +351,6 @@
     shared(DELTA)
     shared(V)
 
-    def grads(j, carry):
-        x = (me.x + 1 + j) % 4
-        delta = jnp.concatenate([jnp.sum(dg[x, 0:8], axis=0), jnp.sum(dg[x, 8:16], axis=0)], axis=1)
-        dp = dot(vg[...].reshape(1024, 128), gg[x], NT)
-        ds = (e[x] * (dp - delta)).astype(BF)
-        dk[...] += dot(ds, qg[x], NN)
-        dq = jnp.transpose(dot(kt[...], ds, NN)) * SCALE
-
-        @pl.when(j == 3)
-        def _():
-            dqo[...] = dq
-
-        @pl.when(j < 3)
-        def _():
-            rss[0, x] = dq.astype(BF)
-            to_sum(0, me.x, x, (me.c, me.yl * 8 + x * 2 + me.k)).start()
-
-        return carry
-
-    lax.fori_loop(0, 4, grads, 0)
-    summed(0, me.x)
-    push_sums(1, dk)
-
     def give(i):
         piece = me.yl * 4 + me.x
         dst = outs.at[
@@ -394,7 +372,7 @@
         drains.append(lambda: pl.when(apart)(lambda: last.wait_send()))
         pend["ret", i] = landed(outs.at[i], ret_r.at[i])
 
-    for i in (2, 0, 1):
+    def settle(i):
         own = me.x if i == 0 else me.y
         if i == 0:
             total = dqo[...]
@@ -406,6 +384,33 @@
             total = total + rsr[i, (own + j) % 4].astype(F32)
         fin[i] = total.astype(BF)
         give(i)
+
+    def grads(j, carry):
+        x = (me.x + 1 + j) % 4
+        delta = jnp.concatenate([jnp.sum(dg[x, 0:8], axis=0), jnp.sum(dg[x, 8:16], axis=0)], axis=1)
+        dp = dot(vg[...].reshape(1024, 128), gg[x], NT)
+        ds = (e[x] * (dp - delta)).astype(BF)
+        dk[...] += dot(ds, qg[x], NN)
+        dq = jnp.transpose(dot(kt[...], ds, NN)) * SCALE
+
+        @pl.when(j == 3)
+        def _():
+            dqo[...] = dq
+
+        @pl.when(j < 3)
+        def _():
+            rss[0, x] = dq.astype(BF)
+            to_sum(0, me.x, x, (me.c, me.yl * 8 + x * 2 + me.k)).start()
+
+        return carry
+
+    lax.fori_loop(0, 4, grads, 0)
+    summed(0, me.x)
+    push_sums(1, dk)
+
+    settle(2)
+    settle(0)
+    settle(1)
     finish()
 
 

time: 75.4 us -> 69 us (0.915)
  the two profiles are of different devices: /device:TPU:9 before, /device:TPU:1 now
where the time goes in v4:
time: 69 us; the launch traced here: 67.8 us
  Pallas kernels  67.1 us (97%)
    pallas_call x1, Pallas kernels, local(): pl.pallas_call(kernel, out_shape=jax.ShapeDtypeStruct((3, 128, 256), BF),...  65.6 us
    pallas_call x1, Pallas kernels, local(): pl.pallas_call(split, out_shape=(shape, shape, shape), in_specs=[any_], o...  1.58 us

profile of v4, /device:TPU:1, one launch (start us, length us, event | category | flops | bytes accessed | tf_op | source)
XLA Modules:
  0.0 67.8 jit_solution(13548991678542027572)
XLA Ops:
  0.6 65.6 %attention_backward.1.a_ref = bf16[3,128,256]{2,1,0:T(8,128)(2,1)} custom-call(bf16[128,256]{1,0:T(8,128)(2,1)} %q_ref.1, bf16[128,256]{1,0:T(8,128)(2,1)} %k_ref.1, bf16[128,256]{1,0:T(8,128)(2,1)} %v_ref.1, bf16[128,256]{1,0:T(8,128)(2,1)} %o_ref.1, bf16[128,384]{1,0:T(8,128)(2,1)} %og_ref.1, bf16[256,6144]{1,0:T(8,128)(2,1)} %w_ref.1, s32[1,128]{1,0:T(1,128)} %bitcast.1), custom_call_target="tpu_custom_call" | custom-call | flops 2000000000 | bytes 4000000 | tf_op jit(solution)/shard_map/attention_backward/pallas_call | solution.py:481
  66.2 1.6 %split_outputs.1 = (bf16[128,256]{1,0:T(8,128)(2,1)}, bf16[128,256]{1,0:T(8,128)(2,1)}, bf16[128,256]{1,0:T(8,128)(2,1)}) custom-call(bf16[3,128,256]{2,1,0:T(8,128)(2,1)} %attention_backward.1.a_ref), custom_call_target="tpu_custom_call" | custom-call | tf_op jit(solution)/shard_map/split_outputs/pallas_call | solution.py:494

commit v5 on v4

--- a/solution.py
+++ b/solution.py
@@ -66,10 +66,10 @@
 
 def kernel(
     q_ref, k_ref, v_ref, o_ref, og_ref, w_ref, tok_ref, out_ref,
-    og, w, qi, ki, vi, oi, gi, brow, drow, dsend, relay, drelay,
+    tok, og, w, qi, ki, vi, oi, gi, brow, drow, dsend, relay, drelay,
     qg, kg, vg, gg, bg, dg, st, e, ms, kt, bt, xb,
     dv, dk, dqo, rss, rsr, fin, outs,
-    word, ld, p0s, p0r, rls, rlr, a2s, a2r, ags, agr, rs_s, rs_r, ret_s, ret_r,
+    word, ld, od, p0s, p0r, rls, rlr, a2s, a2r, ags, agr, rs_s, rs_r, ret_s, ret_r,
 ):
     me = Place()
 
@@ -78,7 +78,6 @@
     def finish():
         for wait in list(pend.values()) + drains:
             wait()
-        out_ref[...] = outs[...]
 
     def remote(src, dst, s, r, d):
         return pltpu.make_async_remote_copy(src, dst, s, r, device_id=d, device_id_type=MESH)
@@ -114,7 +113,7 @@
     loads = [
         pltpu.make_async_copy(src, dst, ld.at[i])
         for i, (src, dst) in enumerate(
-            ((og_ref, mine), (q_ref, qi), (k_ref, ki), (v_ref, vi), (w_ref, w), (o_ref, oi))
+            ((og_ref, mine), (q_ref, qi), (k_ref, ki), (v_ref, vi), (w_ref, w), (o_ref, oi), (tok_ref, tok))
         )
     ]
     for i, c in enumerate(loads):
@@ -124,7 +123,6 @@
     def loaded(i):
         pend.pop(("load", i))()
 
-    brow[...] = jnp.log(tok_ref[...].astype(F32)).astype(BF).astype(F32)
     loaded(0)
     pl.semaphore_wait(barrier, expected)
     tell(0)
@@ -232,6 +230,8 @@
     told(2)
     climb(Q)
     climb(K)
+    loaded(6)
+    brow[...] = jnp.log(tok[...].astype(F32)).astype(BF).astype(F32)
     climb(BIAS)
     acc = lax.fori_loop(1, 8, gather, jnp.zeros((128, 256), F32))
     last = (me.t // 2) ^ 7
@@ -411,6 +411,11 @@
     settle(2)
     settle(0)
     settle(1)
+    for i in (2, 0, 1):
+        pend.pop(("ret", i))()
+        c = pltpu.make_async_copy(outs.at[i], out_ref.at[i], od.at[i])
+        c.start()
+        drains.append(c.wait)
     finish()
 
 
@@ -429,9 +434,9 @@
 
 def local(queries, keys, values, attn_out, out_grad, out_weight, token_sizes):
     any_ = pl.BlockSpec(memory_space=pl.ANY)
-    vmem = pl.BlockSpec(memory_space=pltpu.VMEM)
     dma = pltpu.SemaphoreType.DMA
     scratch = [
+        pltpu.VMEM((1, 128), jnp.int32),
         pltpu.VMEM((128, 6144), BF),
         pltpu.VMEM((256, 6144), BF),
         pltpu.VMEM((128, 256), BF),
@@ -464,7 +469,8 @@
         pltpu.VMEM((3, 256, 128), BF),
         pltpu.VMEM((3, 128, 256), BF),
         pltpu.SemaphoreType.REGULAR((3,)),
-        dma((6,)),
+        dma((7,)),
+        dma((3,)),
         dma((2,)),
         dma((16,)),
         dma((6,)),
@@ -481,8 +487,8 @@
     stacked = pl.pallas_call(
         kernel,
         out_shape=jax.ShapeDtypeStruct((3, 128, 256), BF),
-        in_specs=[any_] * 6 + [vmem],
-        out_specs=vmem,
+        in_specs=[any_] * 7,
+        out_specs=any_,
         scratch_shapes=scratch,
         compiler_params=pltpu.CompilerParams(
             collective_id=0, has_side_effects=True, vmem_limit_bytes=62 * 2**20

time: 69 us -> 68.5 us (level)
  no operation moved by 1% of the time
where the time goes in v5:
time: 68.5 us; the launch traced here: 67.7 us
  Pallas kernels  67.1 us (98%)
    pallas_call x1, Pallas kernels, local(): pl.pallas_call(kernel, out_shape=jax.ShapeDtypeStruct((3, 128, 256), BF),...  65.5 us
    pallas_call x1, Pallas kernels, local(): pl.pallas_call(split, out_shape=(shape, shape, shape), in_specs=[any_], o...  1.58 us

profile of v5, /device:TPU:1, one launch (start us, length us, event | category | flops | bytes accessed | tf_op | source)
XLA Modules:
  0.0 67.7 jit_solution(13716053673441619983)
XLA Ops:
  0.6 65.5 %attention_backward.1.a_ref = bf16[3,128,256]{2,1,0:T(8,128)(2,1)} custom-call(bf16[128,256]{1,0:T(8,128)(2,1)} %q_ref.1, bf16[128,256]{1,0:T(8,128)(2,1)} %k_ref.1, bf16[128,256]{1,0:T(8,128)(2,1)} %v_ref.1, bf16[128,256]{1,0:T(8,128)(2,1)} %o_ref.1, bf16[128,384]{1,0:T(8,128)(2,1)} %og_ref.1, bf16[256,6144]{1,0:T(8,128)(2,1)} %w_ref.1, s32[1,128]{1,0:T(1,128)} %bitcast.1), custom_call_target="tpu_custom_call" | custom-call | flops 2000000000 | bytes 4000000 | tf_op jit(solution)/shard_map/attention_backward/pallas_call | solution.py:487
  66.1 1.6 %split_outputs.1 = (bf16[128,256]{1,0:T(8,128)(2,1)}, bf16[128,256]{1,0:T(8,128)(2,1)}, bf16[128,256]{1,0:T(8,128)(2,1)}) custom-call(bf16[3,128,256]{2,1,0:T(8,128)(2,1)} %attention_backward.1.a_ref), custom_call_target="tpu_custom_call" | custom-call | tf_op jit(solution)/shard_map/split_outputs/pallas_call | solution.py:500

commit v6 on v5

--- a/solution.py
+++ b/solution.py
@@ -90,11 +90,11 @@
     def greet(d):
         pl.semaphore_signal(barrier, inc=1, device_id=d, device_id_type=MESH)
 
-    each(15, lambda i: greet(me.group((me.t + i + 1) % 16)))
     for l in range(2):
         greet((me.z * 2 + 1 - me.yh, l * 8 + me.x * 2 + me.k))
     for j in (1, 15):
         greet(me.column((me.z + j) % 16))
+    each(15, lambda i: greet(me.group((me.t + i + 1) % 16)))
     expected = 19
     apart = me.t != me.z
 

time: 68.5 us -> 68.7 us (level)
  no operation moved by 1% of the time
where the time goes in v6:
time: 68.7 us; the launch traced here: 68.1 us
  Pallas kernels  67.5 us (98%)
    pallas_call x1, Pallas kernels, local(): pl.pallas_call(kernel, out_shape=jax.ShapeDtypeStruct((3, 128, 256), BF),...  65.9 us
    pallas_call x1, Pallas kernels, local(): pl.pallas_call(split, out_shape=(shape, shape, shape), in_specs=[any_], o...  1.58 us

profile of v6, /device:TPU:1, one launch (start us, length us, event | category | flops | bytes accessed | tf_op | source)
XLA Modules:
  0.0 68.1 jit_solution(2038403886958227502)
XLA Ops:
  0.6 65.9 %attention_backward.1.a_ref = bf16[3,128,256]{2,1,0:T(8,128)(2,1)} custom-call(bf16[128,256]{1,0:T(8,128)(2,1)} %q_ref.1, bf16[128,256]{1,0:T(8,128)(2,1)} %k_ref.1, bf16[128,256]{1,0:T(8,128)(2,1)} %v_ref.1, bf16[128,256]{1,0:T(8,128)(2,1)} %o_ref.1, bf16[128,384]{1,0:T(8,128)(2,1)} %og_ref.1, bf16[256,6144]{1,0:T(8,128)(2,1)} %w_ref.1, s32[1,128]{1,0:T(1,128)} %bitcast.1), custom_call_target="tpu_custom_call" | custom-call | flops 2000000000 | bytes 4000000 | tf_op jit(solution)/shard_map/attention_backward/pallas_call | solution.py:487
  66.5 1.6 %split_outputs.1 = (bf16[128,256]{1,0:T(8,128)(2,1)}, bf16[128,256]{1,0:T(8,128)(2,1)}, bf16[128,256]{1,0:T(8,128)(2,1)}) custom-call(bf16[3,128,256]{2,1,0:T(8,128)(2,1)} %attention_backward.1.a_ref), custom_call_target="tpu_custom_call" | custom-call | tf_op jit(solution)/shard_map/split_outputs/pallas_call | solution.py:500
